TPU v7x, 32 devices: a whole 2x2x4 slice. The times are simulated.
32 devices in a mesh: train: 4 (over y, x), roll: 8 (over z, core).
Axes of the slice: x: 2, y: 2, z: 4, core: 2. Of those that a mesh axis runs over, the one named last changes fastest.
Arguments:
- master_gate: float32 [4, 2048, 7168], P(None, 'roll', 'train'), may hold values from -1 to 1
- master_up: float32 [4, 2048, 7168], P(None, 'roll', 'train'), may hold values from -1 to 1
- master_down: float32 [4, 2048, 7168], P(None, 'roll', 'train'), may hold values from -1 to 1
- tokens: bfloat16 [512, 7168], P('roll'), may hold values from -6 to 6
- expert_ids: int32 [512, 2], P('roll'), may hold values from 0 to 3, all different within a row; in each aligned block of 64 rows (0 to 63, 64 to 127, ...) at most 32 rows name the same one
- gate_weights: float32 [512, 2], P('roll'), may hold values from 0.2 to 1
- placement: int32 [8], replicated, may hold values from 0 to 3, as said below
Outputs:
- slot_gate: bfloat16 [8, 16, 128, 7168], P('roll', None, 'train')
- slot_up: bfloat16 [8, 16, 128, 7168], P('roll', None, 'train')
- slot_down: bfloat16 [8, 16, 128, 7168], P('roll', None, 'train')
- mixed_out: bfloat16 [512, 7168], P('roll', 'train')
Inputs may be any that keep to these rules, and one draw needn't show every extreme that they name: `expert_ids`: the 2 experts of a row differ. In each aligned block of 64 rows (the rows of one index of roll) no expert is named by more than 32 rows, a bound that some block reaches. `placement`: every expert of the window is held by exactly two owners.
All inputs are finite; a program needn't handle non-finite values. Where the computation divides by a largest or mean magnitude, that divisor is 1e-20 or more.
Results may differ from a plain program's by a relative error of at most 0.0093.
Values may be sent and summed in bfloat16 or wider, within the bound.
No kernel may reach another device: no remote copies, remote signals or barrier semaphores. Data moves between devices by JAX's collectives and lax.ppermute only.
A program may use at most 256 MiB of HBM per device.

v0:
```python
import functools

import jax
import jax.numpy as jnp
from jax import lax
from jax.experimental import pallas as pl
from jax.experimental.pallas import tpu as pltpu
from jax.sharding import PartitionSpec as P

BLOCK = 128
CORES = 2
VMEM_BYTES = 48 * 1024 * 1024
LIGHT = pl.CostEstimate(flops=1, bytes_accessed=1, transcendentals=0)


def any_spec():
    return pl.BlockSpec(memory_space=pl.ANY)


def smem_spec():
    return pl.BlockSpec(memory_space=pltpu.SMEM)


def quantize_kernel(trains, x_ref, *refs):
    q_ref, d_ref = refs[-2:]
    rows = BLOCK // trains
    features = x_ref.shape[-1]
    for col in range(features // BLOCK):
        cols = slice(col * BLOCK, (col + 1) * BLOCK)
        block = x_ref[0, :, cols]
        peak = jnp.max(jnp.max(jnp.abs(block), axis=0, keepdims=True), axis=1, keepdims=True)
        scale = peak.astype(jnp.bfloat16).astype(jnp.float32)
        quant = (block * (1.0 / scale)).astype(jnp.bfloat16)
        q_ref[:, 0, 0, :, cols] = quant.reshape(trains, rows, BLOCK)
        d_ref[0, 0, :, cols] = (quant.astype(jnp.float32) * scale).astype(jnp.bfloat16)


def quantize(master, first, blocks, trains, slots, base=0, into=None, after=()):
    experts, _, features = master.shape
    rows = BLOCK // trains
    operands = [master] + list(after) + ([] if into is None else [into])
    return pl.pallas_call(
        functools.partial(quantize_kernel, trains),
        grid=(experts, blocks),
        in_specs=[pl.BlockSpec((1, BLOCK, features), lambda e, b: (e, first + b, 0))]
        + [any_spec()] * (len(operands) - 1),
        out_specs=[
            pl.BlockSpec((trains, 1, 1, rows, features), lambda e, b: (0, base + e, b, 0, 0)),
            pl.BlockSpec((1, 1, BLOCK, features), lambda e, b: (e, b, 0, 0)),
        ],
        out_shape=[
            jax.ShapeDtypeStruct((trains, slots, blocks, rows, features), jnp.bfloat16),
            jax.ShapeDtypeStruct((experts, blocks, BLOCK, features), jnp.bfloat16),
        ],
        input_output_aliases={} if into is None else {len(operands) - 1: 0},
        compiler_params=pltpu.CompilerParams(vmem_limit_bytes=VMEM_BYTES),
        cost_estimate=LIGHT,
        name="quantize",
    )(*operands)


def start_choice(plan_ref, arrays, choice, target, sem):
    tests, array, (kind, n, *more) = choice
    ref = arrays[array]
    if kind == "is":
        view = ref.at[n]
    elif kind == "at":
        view = ref.at[plan_ref[n]]
    else:
        view = ref.at[:, plan_ref[n] + more[0], pl.ds(more[1], 1)]
    hit = None
    for place, value in tests:
        test = plan_ref[place] == value
        hit = test if hit is None else hit & test

    def go():
        pltpu.make_async_copy(view, target, sem).start()

    if hit is None:
        go()
    else:
        pl.when(hit)(go)


def pack_kernel(pieces, n_in, plan_ref, *refs):
    arrays = refs[:n_in]
    out, held, sem_in, sem_out = refs[-4:]
    for n, choices in enumerate(pieces):
        for choice in choices:
            start_choice(plan_ref, arrays, choice, held.at[n], sem_in.at[n])
    for n in range(len(pieces)):
        pltpu.make_async_copy(held.at[n], held.at[n], sem_in.at[n]).wait()
        pltpu.make_async_copy(held.at[n], out.at[n], sem_out.at[n]).start()
    for n in range(len(pieces)):
        pltpu.make_async_copy(held.at[n], out.at[n], sem_out.at[n]).wait()


class Arrays:
    def __init__(self):
        self.items = []

    def add(self, array):
        for n, item in enumerate(self.items):
            if item is array:
                return n
        self.items.append(array)
        return len(self.items) - 1


def number_choices(pieces, arrays):
    return [[(tests, arrays.add(a), index) for tests, a, index in choices] for choices in pieces]


def pack(plan, shape, pieces, after=()):
    arrays = Arrays()
    pieces = number_choices(pieces, arrays)
    n_in = len(arrays.items)
    size = len(pieces)
    for dim in shape:
        size *= dim
    operands = arrays.items + list(after)
    return pl.pallas_call(
        functools.partial(pack_kernel, pieces, n_in),
        in_specs=[smem_spec()] + [any_spec()] * len(operands),
        out_specs=any_spec(),
        out_shape=jax.ShapeDtypeStruct((len(pieces),) + shape, jnp.bfloat16),
        scratch_shapes=[
            pltpu.VMEM((len(pieces),) + shape, jnp.bfloat16),
            pltpu.SemaphoreType.DMA((len(pieces),)),
            pltpu.SemaphoreType.DMA((len(pieces),)),
        ],
        compiler_params=pltpu.CompilerParams(vmem_limit_bytes=VMEM_BYTES),
        cost_estimate=LIGHT,
        name="pack",
    )(plan, *operands)


def place_kernel(pieces, sources, first, blocks, n_in, plan_ref, *refs):
    arrays = refs[:n_in]
    out, mark, held, sem_in, sem_out = refs[-5:]
    trains, count, _, features = held.shape[1:]
    for n, choices in enumerate(pieces):
        for choice in choices:
            start_choice(plan_ref, arrays, choice, held.at[n], sem_in.at[n])
    mark[...] = jnp.zeros_like(mark)
    stores = []
    for n in range(len(pieces)):
        pltpu.make_async_copy(held.at[n], held.at[n], sem_in.at[n]).wait()
        start = plan_ref[sources[n]] * blocks + first
        for part in range(trains):
            store = pltpu.make_async_copy(
                held.at[n, part],
                out.at[pl.ds(start, count), :, pl.ds(part * features, features)],
                sem_out.at[n, part],
            )
            store.start()
            stores.append(store)
    for store in stores:
        store.wait()


def place_pieces(plan, shape, owners, pieces, sources, first, blocks, out, after=()):
    trains, count, rows, features = shape
    arrays = Arrays()
    pieces = number_choices(pieces, arrays)
    n_in = len(arrays.items)
    operands = arrays.items + list(after) + ([] if out is None else [out])
    return pl.pallas_call(
        functools.partial(place_kernel, pieces, sources, first, blocks, n_in),
        in_specs=[smem_spec()] + [any_spec()] * len(operands),
        out_specs=[any_spec(), pl.BlockSpec(memory_space=pltpu.VMEM)],
        out_shape=[
            jax.ShapeDtypeStruct((owners * blocks, rows, trains * features), jnp.bfloat16),
            jax.ShapeDtypeStruct((8, BLOCK), jnp.float32),
        ],
        scratch_shapes=[
            pltpu.VMEM((len(pieces),) + shape, jnp.bfloat16),
            pltpu.SemaphoreType.DMA((len(pieces),)),
            pltpu.SemaphoreType.DMA((len(pieces), trains)),
        ],
        input_output_aliases={} if out is None else {len(operands): 0},
        compiler_params=pltpu.CompilerParams(vmem_limit_bytes=VMEM_BYTES),
        cost_estimate=LIGHT,
        name="place_pieces",
    )(plan, *operands)


def plan_places(experts):
    names = [f"send{slot}" for slot in range(experts)]
    names += ["inner", "core", "chip", "side", "own", "mate", "out0", "out1", "most"]
    names += [f"{list_}_{who}" for list_ in ("here", "there") for who in ("own", "mate", "out0", "out1")]
    names += [f"from_{who}{n}" for who in ("own", "mate") for n in range(4)]
    return {name: n for n, name in enumerate(names)}


def plan_kernel(experts, owners, places, me_ref, placement_ref, out_ref):
    me = me_ref[0]
    chip, core = lax.div(me, CORES), lax.rem(me, CORES)
    side = lax.div(chip, 2)
    half = owners // 2
    needs, ranks = [], []
    for s in range(2):
        need = []
        for e in range(experts):
            found = jnp.int32(0)
            for o in range(s * half, (s + 1) * half):
                found = jnp.where(placement_ref[o] == e, 1, found)
            need.append(found)
        rank = []
        for e in range(experts):
            total = jnp.int32(0)
            for other in range(experts):
                if other != e:
                    ahead = need[other] >= need[e] if other < e else need[other] > need[e]
                    total = total + jnp.where(ahead, 1, 0)
            rank.append(total)
        needs.append(sum(need))
        ranks.append(rank)
    here = [jnp.where(side == 0, a, b) for a, b in zip(*ranks)]
    there = [jnp.where(side == 0, b, a) for a, b in zip(*ranks)]
    outer = 3 * side
    values = {
        "inner": jnp.where((chip == 1) | (chip == 2), 1, 0),
        "core": core,
        "chip": chip,
        "side": side,
        "own": placement_ref[me],
        "mate": placement_ref[chip * CORES + 1 - core],
        "out0": placement_ref[outer * CORES],
        "out1": placement_ref[outer * CORES + 1],
        "most": jnp.maximum(*needs),
    }
    for slot in range(experts):
        values[f"send{slot}"] = sum(jnp.where(there[e] == slot, e, 0) for e in range(experts))
    for who in ("own", "mate", "out0", "out1"):
        for list_, rank in (("here", here), ("there", there)):
            values[f"{list_}_{who}"] = sum(
                jnp.where(values[who] == e, rank[e], 0) for e in range(experts)
            )
    for n, source in enumerate((chip, 1 + 4 * side - chip, 2 - side, 3 - 3 * side)):
        values[f"from_own{n}"] = source * CORES + core
        values[f"from_mate{n}"] = source * CORES + 1 - core
    for name, n in places.items():
        out_ref[n] = values[name]


def make_plan(placement, experts, owners, after=()):
    places = plan_places(experts)
    me = jnp.reshape(lax.axis_index("roll"), (1,)).astype(jnp.int32)
    plan = pl.pallas_call(
        lambda *refs: plan_kernel(experts, owners, places, refs[0], refs[1], refs[-1]),
        in_specs=[smem_spec(), smem_spec()] + [any_spec()] * len(after),
        out_specs=smem_spec(),
        out_shape=jax.ShapeDtypeStruct((len(places),), jnp.int32),
        cost_estimate=LIGHT,
        name="plan",
    )(me, placement, *after)
    return plan, places


def line_schedule(opens, experts, cap, ride_from):
    chunks = range(len(opens))
    own, far = list(chunks), list(chunks)
    fresh = [("x", c, i) for c in chunks for i in range(CORES)]
    near = [("near", c, s) for c in chunks for s in range(cap, experts)]
    middle, inwards, outwards = [], [], []
    arrived, relayed, ride_due = [], [], {"in": ride_from}
    n = 0
    while own or arrived or far or near or fresh or relayed or ride_due:
        across, ins, outs = [], [], []
        if arrived and arrived[0][0] <= n:
            c = arrived.pop(0)[1]
            across = [("far", c, s) for s in range(cap)]
        elif own and opens[own[0]] <= n:
            c = own.pop(0)
            across = [("own", c, s) for s in range(cap)]
        if across:
            relayed += [(n + 2, (across[0][0], c, i)) for i in range(CORES)]
        if ride_due.get("across", n + 1) <= n and (not across or across[0][0] == "own"):
            across.append(("ride", 0, 0))
            del ride_due["across"]
            ride_due["out"] = n + 2
        if far and opens[far[0]] <= n:
            c = far.pop(0)
            ins = [("far", c, s) for s in range(cap)]
            arrived.append((n + 2, c))
        else:
            if ride_due.get("in", n + 1) <= n:
                ins = [("ride", 0, 0), ("ride", 0, 1)]
                del ride_due["in"]
                ride_due["across"] = n + 2
            while near and opens[near[0][1]] <= n and len(ins) < cap:
                ins.append(near.pop(0))
        while relayed and relayed[0][0] <= n and len(outs) < cap:
            outs.append(relayed.pop(0)[1])
        if ride_due.get("out", n + 1) <= n and len(outs) < cap:
            outs.append(("ride", 0, 0))
            del ride_due["out"]
        while fresh and opens[fresh[0][1]] <= n and len(outs) < cap:
            outs.append(fresh.pop(0))
        middle.append(across)
        inwards.append(ins)
        outwards.append(outs)
        n += 1
    return middle, inwards, outwards


def link_pairs(chip_pairs, swap_chips=()):
    pairs = []
    for core in range(CORES):
        for a, b in chip_pairs:
            pairs.append((a * CORES + core, b * CORES + core))
        for chip in swap_chips:
            pairs.append((chip * CORES + core, chip * CORES + 1 - core))
    return pairs


EDGES = ((0, 1), (1, 0), (2, 3), (3, 2))


def line_exchange(x_first, quant_rest, dequant, plan, places, routed, shapes, cap):
    experts, blocks, trains, owners = shapes
    features = x_first.shape[-1]
    rows = BLOCK // trains
    shape = (trains, 1, rows, features)
    chunks = [(m, b) for m in range(3) for b in range(blocks)]
    count = len(chunks)
    opens = [(0, 2, 5)[m] for m, _ in chunks]
    ride_from = 8
    middle, inwards, outwards = line_schedule(opens, experts, cap, ride_from)
    rounds = len(outwards)
    last_far = max(n for n in range(rounds) if inwards[n] and inwards[n][0][0] == "far")
    edge_pairs = link_pairs(EDGES)
    middle_pairs = link_pairs([(1, 2), (2, 1)], swap_chips=(0, 3))
    swap_pairs = link_pairs([], swap_chips=range(4))
    is_inner, is_outer = (places["inner"], 1), (places["inner"], 0)
    on_core = [(places["core"], core) for core in range(CORES)]
    got_edge, got_middle, where = {}, {}, {}
    last = [x_first]

    xs = [x_first] + [
        lax.all_to_all(quant, "train", split_axis=0, concat_axis=0, tiled=True)
        for quant in quant_rest
    ]

    def local(c, name):
        m, b = chunks[c]
        return xs[m], ("expert", places[name], 0, b)

    def packed(pieces, after=()):
        last[0] = pack(plan, shape, pieces, [last[0]] + list(after))
        return last[0]

    ready = {(c, 0): opens[c] for c in range(count)}

    def note(c, position, n):
        ready[c, position] = max(ready.get((c, position), 0), n)

    from_kind = {"x": 1, "own": 2, "far": 3}
    kind_of = {position: kind for kind, position in from_kind.items()}
    for n in range(rounds):
        for i, piece in enumerate(middle[n]):
            where[("across",) + piece] = (n, i)
            if piece[0] != "ride":
                note(piece[1], 2 if piece[0] == "own" else 3, n)
        for i, piece in enumerate(inwards[n]):
            where[("in",) + piece] = (n, i)
            if piece[0] != "ride":
                note(piece[1], 1, n)
        for i, piece in enumerate(outwards[n]):
            where[("out",) + piece] = (n, i)
            if piece[0] != "ride":
                note(piece[1], from_kind[piece[0]], n)

    def across(kind, c):
        return got_middle[where["across", kind, c, 0][0]]

    def find(c, position, who):
        if position == 0:
            return [((),) + local(c, who)]
        choices = []
        if position == 1:
            for slot in range(experts):
                n, i = where["in", "far" if slot < cap else "near", c, slot]
                test = (places[f"there_{who}"], slot)
                choices.append(((is_inner, test), got_edge[n], ("is", i)))
        else:
            got = across(kind_of[position], c)
            choices.append(((is_inner,), got, ("at", places[f"here_{who}"])))
        for core in range(CORES):
            n, i = where["out", kind_of[position], c, core if who == "own" else 1 - core]
            choices.append(((is_outer, on_core[core]), got_edge[n], ("is", i)))
        return choices

    to_swap = sorted((ready[c, p], c, p) for c in range(count) for p in range(4))
    to_place = []
    outs = [None, None, None]

    def swap(n, by):
        taken = []
        while to_swap and to_swap[0][0] <= by and len(taken) < 3:
            taken.append(to_swap.pop(0))
        if taken:
            got = lax.ppermute(
                packed([find(c, p, "mate") for _, c, p in taken]), "roll", swap_pairs
            )
            to_place.append((n, got, [(c, p) for _, c, p in taken]))
        return bool(taken)

    def place(got, taken):
        for c in sorted({c for c, _ in taken}):
            m, b = chunks[c]
            here = [(i, p) for i, (other, p) in enumerate(taken) if other == c]
            pieces = [find(c, p, "own") for _, p in here]
            pieces += [[((), got, ("is", i))] for i, _ in here]
            sources = [places[f"from_own{p}"] for _, p in here]
            sources += [places[f"from_mate{p}"] for _, p in here]
            outs[m], last[0] = place_pieces(
                plan, shape, owners, pieces, sources, b, blocks, outs[m], (last[0],)
            )

    ride = {}
    tokens, ids, weights = routed
    ups, down = dequant[:-1], dequant[-1]

    def ride_first():
        pre, columns = None, 2 * blocks
        for restored in ups:
            for b in range(restored.shape[1]):
                column = 0 if pre is None else column + 1
                pre = pre_activations(tokens, ids, restored, b, pre, column, columns, (last[0],))
                last[0] = pre
        ride["pre"] = lax.psum(pre, "train")
    def ride_mix():
        ride["keep"], going = mix_experts(
            ride["pre"], ids, weights, down, plan, places, (last[0],)
        )
        last[0] = ride["keep"]
        going = going.reshape((-1,) + shape)
        ride["swapped"] = lax.ppermute(going, "roll", swap_pairs)

    def ride_cores():
        got = ride["swapped"].reshape(-1, features)
        ride["sums"], going = sum_cores(plan, places, ride["keep"], got, (last[0],))
        last[0] = ride["sums"]
        ride["in"] = going.reshape((-1,) + shape)

    def ride_in():
        n, i = where["in", "ride", 0, 0]
        got = got_edge[n].reshape(-1, BLOCK, features)
        ride["inner"], going = sum_inwards(plan, places, ride["sums"], got, i, (last[0],))
        last[0] = ride["inner"]
        ride["across"] = going.reshape((-1,) + shape)

    def ride_across():
        n, i = where["across", "ride", 0, 0]
        got = got_middle[n].reshape(-1, BLOCK, features)
        ride["final"], going = sum_across(
            plan, places, ride["sums"], ride["inner"], got, i, (last[0],)
        )
        last[0] = ride["final"]
        ride["out"] = going.reshape((-1,) + shape)

    def ride_out():
        n, i = where["out", "ride", 0, 0]
        got = got_edge[n].reshape(-1, BLOCK, features)
        ride["mixed"] = sum_outwards(
            plan, places, ride["sums"], ride["final"], got, i, (last[0],)
        )
        last[0] = ride["mixed"]

    spare = local(0, "own")
    for n in range(rounds):
        swap(n, n - 2)
        if middle[n]:
            if where.get(("across", "ride", 0, 0), (-1,))[0] == n:
                ride_in()
            pieces = []
            for kind, c, slot in middle[n]:
                if kind == "own":
                    pieces.append([((),) + local(c, f"send{slot}")])
                elif kind == "ride":
                    pieces.append([((), ride["across"], ("is", 0))])
                else:
                    m, i = where["in", kind, c, slot]
                    pieces.append([((), got_edge[m], ("is", i))])
            after = [got_middle[n - 2]] if n - 2 in got_middle else []
            got_middle[n] = lax.ppermute(packed(pieces, after), "roll", middle_pairs)
        if where["out", "ride", 0, 0][0] == n:
            ride_across()
        pieces = []
        for i in range(max(len(inwards[n]), len(outwards[n]))):
            choices = [((is_inner,),) + spare, ((is_outer,),) + spare]
            if i < len(outwards[n]):
                kind, c, core = outwards[n][i]
                if kind == "x":
                    choices[0] = ((is_inner,),) + local(c, f"out{core}")
                elif kind == "ride":
                    choices[0] = ((is_inner,), ride["out"], ("is", 0))
                else:
                    index = ("at", places[f"here_out{core}"])
                    choices[0] = ((is_inner,), across(kind, c), index)
            if i < len(inwards[n]):
                kind, c, slot = inwards[n][i]
                if kind == "ride":
                    choices[1] = ((is_outer,), ride["in"], ("is", slot))
                else:
                    choices[1] = ((is_outer,),) + local(c, f"send{slot}")
            pieces.append(choices)
        while n < last_far and len(pieces) < cap:
            pieces.append([((),) + spare])
        if pieces:
            after = [got_edge[n - 2]] if n - 2 in got_edge else []
            got_edge[n] = lax.ppermute(packed(pieces, after), "roll", edge_pairs)
        if n == 0:
            ride_first()
        if n == ride_from - 3:
            ride_mix()
        if n == ride_from - 1:
            ride_cores()
        if n == where["out", "ride", 0, 0][0] + 2:
            ride_out()
        while to_place and to_place[0][0] <= n - 2:
            place(*to_place.pop(0)[1:])
    while to_swap:
        early = list(to_place)
        del to_place[:]
        swap(rounds, to_swap[0][0])
        for _, got, taken in early:
            place(got, taken)
    if "mixed" not in ride:
        ride_out()
    for _, got, taken in to_place:
        place(got, taken)
    return tuple(outs) + (ride["mixed"],)


def direct_exchange(quants, placement, trains, owners):
    outs = []
    for quant in quants:
        _, experts, blocks, rows, features = quant.shape
        x = lax.all_to_all(quant, "train", split_axis=0, concat_axis=0, tiled=True)
        x = jnp.transpose(x, (1, 2, 3, 0, 4)).reshape(experts, blocks, rows, trains * features)
        picked = jnp.take(x, placement, axis=0)
        got = lax.all_to_all(picked, "roll", split_axis=0, concat_axis=0, tiled=True)
        outs.append(got.reshape(owners * blocks, rows, trains * features))
    return outs


def pre_activation_kernel(experts, top, tok_ref, ids_ref, w_ref, *refs):
    out_ref = refs[-1]
    features = tok_ref.shape[1]
    weights = w_ref[...].reshape(experts * BLOCK, features)
    pre = lax.dot_general(
        tok_ref[...], weights, (((1,), (1,)), ((), ())), preferred_element_type=jnp.float32
    )
    for k in range(top):
        total = jnp.zeros((pre.shape[0], BLOCK), jnp.float32)
        for expert in range(experts):
            part = pre[:, expert * BLOCK : (expert + 1) * BLOCK]
            total = total + jnp.where(ids_ref[:, k : k + 1] == expert, part, 0.0)
        out_ref[:, k * BLOCK : (k + 1) * BLOCK] = total


def pre_activations(tokens, ids, restored, block, out, column, columns, after=()):
    count, features = tokens.shape
    experts, top = restored.shape[0], ids.shape[1]
    tile = min(count, 2 * BLOCK)
    operands = [tokens, ids, restored] + list(after) + ([] if out is None else [out])
    return pl.pallas_call(
        functools.partial(pre_activation_kernel, experts, top),
        grid=(count // tile,),
        in_specs=[
            pl.BlockSpec((tile, features), lambda i: (i, 0)),
            pl.BlockSpec((tile, top), lambda i: (i, 0)),
            pl.BlockSpec((experts, 1, BLOCK, features), lambda i: (0, block, 0, 0)),
        ]
        + [any_spec()] * (len(operands) - 3),
        out_specs=pl.BlockSpec((tile, top * BLOCK), lambda i: (i, column)),
        out_shape=jax.ShapeDtypeStruct((count, columns * top * BLOCK), jnp.float32),
        input_output_aliases={} if out is None else {len(operands) - 1: 0},
        compiler_params=pltpu.CompilerParams(vmem_limit_bytes=VMEM_BYTES),
        cost_estimate=LIGHT,
        name="pre_activations",
    )(*operands)


def mix_rows(experts, top, blocks, pre_ref, ids_ref, weights_ref, down_ref):
    width = top * BLOCK
    count, features = ids_ref.shape[0], down_ref.shape[-1]
    hidden = {}
    for b in range(blocks):
        for k in range(top):
            start = b * width + k * BLOCK
            gate = pre_ref[:, start : start + BLOCK]
            up = pre_ref[:, blocks * width + start : blocks * width + start + BLOCK]
            value = gate / (1.0 + jnp.exp(-gate)) * up
            hidden[b, k] = value.astype(jnp.bfloat16).astype(jnp.float32)
    total = jnp.zeros((count, features), jnp.float32)
    for expert in range(experts):
        weight = jnp.zeros((count, 1), jnp.float32)
        for k in range(top):
            weight = weight + jnp.where(
                ids_ref[:, k : k + 1] == expert, weights_ref[:, k : k + 1], 0.0
            )
        value = jnp.zeros((count, features), jnp.float32)
        for b in range(blocks):
            routed = jnp.zeros((count, BLOCK), jnp.float32)
            for k in range(top):
                routed = routed + jnp.where(ids_ref[:, k : k + 1] == expert, hidden[b, k], 0.0)
            value = value + jnp.dot(
                routed.astype(jnp.bfloat16), down_ref[expert, b], preferred_element_type=jnp.float32
            )
        total = total + weight * value
    return total


def mix_kernel(sizes, pre_ref, ids_ref, weights_ref, down_ref, out_ref):
    out_ref[...] = mix_rows(*sizes, pre_ref, ids_ref, weights_ref, down_ref)


def mix_split_kernel(sizes, core, pre_ref, ids_ref, weights_ref, down_ref, plan_ref, *refs):
    keep_ref, send_ref = refs[-2:]
    total = mix_rows(*sizes, pre_ref, ids_ref, weights_ref, down_ref)
    half = total.shape[0] // CORES
    first = plan_ref[core] == 0
    keep_ref[0] = jnp.where(first, total[:half], total[half:])
    send_ref[...] = jnp.where(first, total[half:], total[:half]).astype(send_ref.dtype)


def mix_specs(pre, ids, down, tile):
    return [
        pl.BlockSpec((tile, pre.shape[1]), lambda i: (i, 0)),
        pl.BlockSpec((tile, ids.shape[1]), lambda i: (i, 0)),
        pl.BlockSpec((tile, ids.shape[1]), lambda i: (i, 0)),
        pl.BlockSpec(down.shape, lambda i: (0, 0, 0, 0)),
    ]


def mix_experts(pre, ids, weights, down, plan=None, places=None, after=()):
    count, top = ids.shape
    experts, blocks, _, features = down.shape
    sizes = (experts, top, blocks)
    tile = min(count, BLOCK)
    params = pltpu.CompilerParams(vmem_limit_bytes=VMEM_BYTES)
    if plan is None:
        return pl.pallas_call(
            functools.partial(mix_kernel, sizes),
            grid=(count // tile,),
            in_specs=mix_specs(pre, ids, down, tile),
            out_specs=pl.BlockSpec((tile, features), lambda i: (i, 0)),
            out_shape=jax.ShapeDtypeStruct((count, features), jnp.float32),
            compiler_params=params,
            cost_estimate=LIGHT,
            name="mix_experts",
        )(pre, ids, weights, down)
    half = tile // CORES
    return pl.pallas_call(
        functools.partial(mix_split_kernel, sizes, places["core"]),
        grid=(count // tile,),
        in_specs=mix_specs(pre, ids, down, tile) + [smem_spec()] + [any_spec()] * len(after),
        out_specs=[
            pl.BlockSpec((1, half, features), lambda i: (i, 0, 0)),
            pl.BlockSpec((half, features), lambda i: (i, 0)),
        ],
        out_shape=[
            jax.ShapeDtypeStruct((count // tile, half, features), jnp.float32),
            jax.ShapeDtypeStruct((count // CORES, features), jnp.bfloat16),
        ],
        compiler_params=params,
        cost_estimate=LIGHT,
        name="mix_experts",
    )(pre, ids, weights, down, plan, *after)


def sum_call(kernel, name, out_shape, plan, arrays, piece, after):
    vmem = pl.BlockSpec(memory_space=pltpu.VMEM)
    operands = [plan] + list(arrays)
    specs = [smem_spec()] + [vmem] * len(arrays)
    if piece is not None:
        array, first, number = piece
        operands += [array] * number
        for n in range(number):
            specs.append(
                pl.BlockSpec((1,) + array.shape[1:], lambda i, n=n: (first + n, 0, 0))
            )
    return pl.pallas_call(
        kernel,
        grid=(1,),
        in_specs=specs + [any_spec()] * len(after),
        out_specs=[vmem] * len(out_shape) if isinstance(out_shape, list) else vmem,
        out_shape=out_shape,
        compiler_params=pltpu.CompilerParams(vmem_limit_bytes=VMEM_BYTES),
        cost_estimate=LIGHT,
        name=name,
    )(*operands, *after)


def sum_cores_kernel(places, plan_ref, keep_ref, got_ref, *refs):
    sums_ref, send_ref = refs[-2:]
    chips, tokens, features = keep_ref.shape
    for chip in range(chips):
        rows = slice(chip * tokens, (chip + 1) * tokens)
        sums_ref[chip] = keep_ref[chip] + got_ref[rows, :].astype(jnp.float32)
    side, chip = plan_ref[places["side"]], plan_ref[places["chip"]]
    for n in range(2):
        send_ref[n * tokens : (n + 1) * tokens, :] = sums_ref[2 * (1 - side) + n].astype(
            send_ref.dtype
        )
    partner = sums_ref[1 + 4 * side - chip].astype(send_ref.dtype)
    for n in range(2, 4):
        send_ref[n * tokens : (n + 1) * tokens, :] = partner


def sum_cores(plan, places, keep, got, after=()):
    _, tokens, features = keep.shape
    out_shape = [
        jax.ShapeDtypeStruct(keep.shape, jnp.float32),
        jax.ShapeDtypeStruct((4 * tokens, features), jnp.bfloat16),
    ]
    kernel = functools.partial(sum_cores_kernel, places)
    return sum_call(kernel, "sum_cores", out_shape, plan, [keep, got], None, after)


def sum_inwards_kernel(places, plan_ref, sums_ref, over_ref, here_ref, *refs):
    inner_ref, send_ref = refs[-2:]
    tokens = inner_ref.shape[0]
    side, chip = plan_ref[places["side"]], plan_ref[places["chip"]]
    for n in range(2):
        rows = slice(n * tokens, (n + 1) * tokens)
        total = sums_ref[2 * (1 - side) + n] + over_ref[0, rows, :].astype(jnp.float32)
        send_ref[rows, :] = total.astype(send_ref.dtype)
    inner_ref[...] = sums_ref[chip] + here_ref[0, :tokens, :].astype(jnp.float32)


def sum_inwards(plan, places, sums, got, first, after=()):
    _, tokens, features = sums.shape
    out_shape = [
        jax.ShapeDtypeStruct((tokens, features), jnp.float32),
        jax.ShapeDtypeStruct((2 * tokens, features), jnp.bfloat16),
    ]
    kernel = functools.partial(sum_inwards_kernel, places)
    return sum_call(kernel, "sum_inwards", out_shape, plan, [sums], (got, first, 2), after)


def sum_across_kernel(places, plan_ref, sums_ref, inner_ref, got_ref, *refs):
    final_ref, send_ref = refs[-2:]
    tokens = inner_ref.shape[0]
    side, chip = plan_ref[places["side"]], plan_ref[places["chip"]]
    place = chip - 2 * side
    low = got_ref[0, :tokens, :].astype(jnp.float32)
    high = got_ref[0, tokens:, :].astype(jnp.float32)
    final_ref[...] = inner_ref[...] + jnp.where(place == 0, low, high)
    total = sums_ref[1 + 4 * side - chip] + jnp.where(place == 0, high, low)
    for n in range(2):
        send_ref[n * tokens : (n + 1) * tokens, :] = total.astype(send_ref.dtype)


def sum_across(plan, places, sums, inner, got, first, after=()):
    _, tokens, features = sums.shape
    out_shape = [
        jax.ShapeDtypeStruct((tokens, features), jnp.float32),
        jax.ShapeDtypeStruct((2 * tokens, features), jnp.bfloat16),
    ]
    kernel = functools.partial(sum_across_kernel, places)
    return sum_call(kernel, "sum_across", out_shape, plan, [sums, inner], (got, first, 1), after)


def sum_outwards_kernel(places, plan_ref, sums_ref, final_ref, got_ref, *refs):
    out_ref = refs[-1]
    tokens = final_ref.shape[0]
    outer = sums_ref[plan_ref[places["chip"]]] + got_ref[0, :tokens, :].astype(jnp.float32)
    out_ref[...] = jnp.where(plan_ref[places["inner"]] == 1, final_ref[...], outer).astype(
        out_ref.dtype
    )


def sum_outwards(plan, places, sums, final, got, first, after=()):
    out_shape = jax.ShapeDtypeStruct(final.shape, jnp.bfloat16)
    kernel = functools.partial(sum_outwards_kernel, places)
    return sum_call(kernel, "sum_outwards", out_shape, plan, [sums, final], (got, first, 1), after)


def gather_tokens(tokens, expert_ids, gate_weights, features):
    mine = lax.dynamic_slice_in_dim(tokens, lax.axis_index("train") * features, features, axis=1)
    top = expert_ids.shape[1]
    high = lax.reduce_precision(gate_weights, 8, 7)
    middle = lax.reduce_precision(gate_weights - high, 8, 7)
    low = gate_weights - high - middle
    beside = jnp.concatenate((expert_ids.astype(jnp.float32), high, middle, low), axis=1)
    beside = jnp.pad(beside, ((0, 0), (0, BLOCK - 4 * top))).astype(jnp.bfloat16)
    every = lax.all_gather(jnp.concatenate((mine, beside), axis=1), "roll", axis=0, tiled=True)
    side = every[:, features : features + 4 * top].astype(jnp.float32)
    ids = side[:, :top].astype(jnp.int32)
    weights = side[:, top : 2 * top] + side[:, 2 * top : 3 * top] + side[:, 3 * top :]
    return every[:, :features], ids, weights


def per_device(master_gate, master_up, master_down, tokens, expert_ids, gate_weights, placement):
    trains = lax.axis_size("train")
    owners = lax.axis_size("roll")
    experts, hidden_rows, features = master_gate.shape
    blocks = hidden_rows // BLOCK
    if owners // CORES == 4 and CORES * tokens.shape[0] == BLOCK:
        quant, gate = quantize(master_gate, 0, blocks, trains, experts)
        x_first = lax.all_to_all(quant, "train", split_axis=0, concat_axis=0, tiled=True)
        plan, places = make_plan(placement, experts, owners, (quant,))
        rest_up, up = quantize(master_up, 0, blocks, trains, experts, 0, None, (plan,))
        rest_down, down = quantize(master_down, 0, blocks, trains, experts, 0, None, (rest_up,))
        rest = (rest_up, rest_down)
        dequant = (gate, up, down)
        routed = gather_tokens(tokens, expert_ids, gate_weights, features)
        most = min(experts, owners // 2)
        shapes = (experts, blocks, trains, owners)

        def branch(cap, x_first, rest, dequant, plan, routed):
            return line_exchange(x_first, rest, dequant, plan, places, routed, shapes, cap)

        outs = lax.cond(
            plan[places["most"]] <= most - 1,
            functools.partial(branch, most - 1),
            functools.partial(branch, most),
            x_first,
            rest,
            dequant,
            plan,
            routed,
        )
    else:
        masters = (master_gate, master_up, master_down)
        quants, dequant = zip(*[quantize(w, 0, blocks, trains, experts) for w in masters])
        every, ids, weights = gather_tokens(tokens, expert_ids, gate_weights, features)
        outs = direct_exchange(quants, placement, trains, owners)
        pre = None
        for n in range(2 * blocks):
            restored = dequant[n // blocks]
            pre = pre_activations(every, ids, restored, n % blocks, pre, n, 2 * blocks)
        mixed = mix_experts(lax.psum(pre, "train"), ids, weights, dequant[2])
        mixed = lax.psum_scatter(mixed, "roll", scatter_dimension=0, tiled=True)
        outs = tuple(outs) + (mixed.astype(jnp.bfloat16),)
    return tuple(out[None] for out in outs[:3]) + (outs[3],)


def solution(mesh):
    in_specs = (
        P(None, "roll", "train"),
        P(None, "roll", "train"),
        P(None, "roll", "train"),
        P("roll", None),
        P("roll", None),
        P("roll", None),
        P(),
    )
    out_specs = (
        P("roll", None, "train", None),
        P("roll", None, "train", None),
        P("roll", None, "train", None),
        P("roll", "train"),
    )
    return jax.shard_map(
        per_device, mesh=mesh, in_specs=in_specs, out_specs=out_specs, check_vma=False
    )
```

profile of v0, /device:TPU:19, one launch (start us, length us, event | category | flops | bytes accessed | tf_op | source)
XLA Modules:
  0.0 485.8 jit_solution(104012849156401489)
XLA Ops:
  9.6 8.3 %quantize.3 = (bf16[4,4,2,32,1792]{4,3,2,1,0:T(8,128)(2,1)S(1)}, bf16[4,2,128,1792]{3,2,1,0:T(8,128)(2,1)}) custom-call(f32[4,256,1792]{2,1,0:T(8,128)} %x_ref.3), custom_call_target="tpu_custom_call" | custom-call | flops 1 | bytes 1 | tf_op jit(solution)/shard_map/quantize/pallas_call | solution.py:42
  26.0 8.3 %quantize.4 = (bf16[4,4,2,32,1792]{4,3,2,1,0:T(8,128)(2,1)S(1)}, bf16[4,2,128,1792]{3,2,1,0:T(8,128)(2,1)}) custom-call(f32[4,256,1792]{2,1,0:T(8,128)} %x_ref.4, s32[29]{0:T(128)S(1)} %plan.1.refs_0_), custom_call_target="tpu_custom_call" | custom-call | flops 1 | bytes 1 | tf_op jit(solution)/shard_map/quantize/pallas_call | solution.py:42
  34.3 9.8 %quantize.5 = (bf16[4,4,2,32,1792]{4,3,2,1,0:T(8,128)(2,1)}, bf16[4,2,128,1792]{3,2,1,0:T(8,128)(2,1)}) custom-call(f32[4,256,1792]{2,1,0:T(8,128)} %x_ref.5, bf16[4,4,2,32,1792]{4,3,2,1,0:T(8,128)(2,1)S(1)} %get-tuple-element.173.refs_0_), custom_call_target="tpu_custom_call" | custom-call | flops 1 | bytes 1 | tf_op jit(solution)/shard_map/quantize/pallas_call | solution.py:42
  50.1 15.5 %all-to-all-done.4 = bf16[4,4,2,32,1792]{4,3,2,1,0:T(8,128)(2,1)} async-done(((bf16[4,4,2,32,1792]{4,3,2,1,0:T(8,128)(2,1)}), bf16[4,4,2,32,1792]{4,3,2,1,0:T(8,128)(2,1)}, u32[]{:S(2)}, u32[]{:S(2)}) %all-to-all-start.4) | async-done | bytes 3670048 | tf_op jit(solution)/shard_map/all_to_all | solution.py:806
  65.6 412.2 %conditional.1 = (bf16[16,32,7168]{2,1,0:T(8,128)(2,1)}, bf16[16,32,7168]{2,1,0:T(8,128)(2,1)}, bf16[16,32,7168]{2,1,0:T(8,128)(2,1)}, bf16[64,1792]{1,0:T(8,128)(2,1)}) conditional(s32[]{:T(128)} %bitcast.17, (s32[29]{0:T(128)S(1)}, bf16[4,4,2,32,1792]{4,3,2,1,0:T(8,128)(2,1)}, bf16[512,1792]{1,0:T(8,128)(2,1)}, s32[512,2]{1,0:T(8,128)S(1)}, ...), branch_computations={%region_0.2_spmd, %region_2.4_spmd} | conditional | flops 524358 | bytes 486034240 | solution.py:819
  95.5 15.4 %all-to-all-done.2.refs_1_.refs_2_.refs_0_ = bf16[4,4,2,32,1792]{4,3,2,1,0:T(8,128)(2,1)} async-done(((bf16[4,4,2,32,1792]{4,3,2,1,0:T(8,128)(2,1)}), bf16[4,4,2,32,1792]{4,3,2,1,0:T(8,128)(2,1)}, u32[]{:S(2)}, u32[]{:S(2)}) %all-to-all-start.2) | async-done | bytes 3670048 | tf_op jit(solution)/shard_map/cond/branch_1_fun/all_to_all | solution.py:342
  110.9 5.9 %all-to-all-start.3 = ((bf16[4,4,2,32,1792]{4,3,2,1,0:T(8,128)(2,1)}), bf16[4,4,2,32,1792]{4,3,2,1,0:T(8,128)(2,1)}, u32[]{:S(2)}, u32[]{:S(2)}) async-start(bf16[4,4,2,32,1792]{4,3,2,1,0:T(8,128)(2,1)} %get-tuple-element.102), calls=%async_computation.3 | async-start | bytes 7340032 | tf_op jit(solution)/shard_map/cond/branch_1_fun/all_to_all | solution.py:342
  125.8 10.4 %collective-permute-done.41.refs_0_.refs_3_ = bf16[3,4,1,32,1792]{4,3,2,1,0:T(8,128)(2,1)} collective-permute-done((bf16[3,4,1,32,1792]{4,3,2,1,0:T(8,128)(2,1)}, bf16[3,4,1,32,1792]{4,3,2,1,0:T(8,128)(2,1)}, u32[]{:S(2)}, u32[]{:S(2)}) %collective-permute-start.41) | collective-permute-done | bytes 1376288 | tf_op jit(solution)/shard_map/cond/branch_1_fun/ppermute | solution.py:514
  143.1 5.5 %collective-permute-start.47 = (bf16[2,4,1,32,1792]{4,3,2,1,0:T(8,128)(2,1)}, bf16[2,4,1,32,1792]{4,3,2,1,0:T(8,128)(2,1)}, u32[]{:S(2)}, u32[]{:S(2)}) collective-permute-start(bf16[2,4,1,32,1792]{4,3,2,1,0:T(8,128)(2,1)} %pack.123.refs_1_), channel_id=1, source_target_pairs={{0,1},{2,3},{4,5},{6,7},{1,0},{3,2},{5,4},{7,6},{8,9},{10,11},{12,... | collective-permute-start | bytes 2752520 | tf_op jit(solution)/shard_map/cond/branch_1_fun/ppermute | solution.py:404
  148.6 17.2 %collective-permute-done.49.refs_1_.refs_0_.refs_4_ = bf16[3,4,1,32,1792]{4,3,2,1,0:T(8,128)(2,1)S(1)} collective-permute-done((bf16[3,4,1,32,1792]{4,3,2,1,0:T(8,128)(2,1)}, bf16[3,4,1,32,1792]{4,3,2,1,0:T(8,128)(2,1)S(1)}, u32[]{:S(2)}, u32[]{:S(2)}) %collective-permute-start.49) | collective-permute-done | bytes 1376288 | tf_op jit(solution)/shard_map/cond/branch_1_fun/ppermute | solution.py:514
  175.3 5.4 %collective-permute-start.52 = (bf16[3,4,1,32,1792]{4,3,2,1,0:T(8,128)(2,1)}, bf16[3,4,1,32,1792]{4,3,2,1,0:T(8,128)(2,1)}, u32[]{:S(2)}, u32[]{:S(2)}) collective-permute-start(bf16[3,4,1,32,1792]{4,3,2,1,0:T(8,128)(2,1)} %pack.128.refs_1_), channel_id=1, source_target_pairs={{0,1},{2,3},{4,5},{6,7},{1,0},{3,2},{5,4},{7,6},{8,9},{10,11},{12,... | collective-permute-start | bytes 4128776 | tf_op jit(solution)/shard_map/cond/branch_1_fun/ppermute | solution.py:404
  185.8 9.4 %collective-permute-done.46.refs_1_.refs_0_.refs_4_.refs_2_ = bf16[3,4,1,32,1792]{4,3,2,1,0:T(8,128)(2,1)S(1)} collective-permute-done((bf16[3,4,1,32,1792]{4,3,2,1,0:T(8,128)(2,1)}, bf16[3,4,1,32,1792]{4,3,2,1,0:T(8,128)(2,1)S(1)}, u32[]{:S(2)}, u32[]{:S(2)}) %collective-permute-start.46) | collective-permute-done | bytes 1376288 | tf_op jit(solution)/shard_map/cond/branch_1_fun/ppermute | solution.py:514
  203.0 17.8 %all-reduce.6.cloned.1.call-done.pre_ref = f32[512,1024]{1,0:T(8,128)} async-done(((f32[512,1024]{1,0:T(8,128)}), f32[512,1024]{1,0:T(8,128)}) %all-reduce.6.cloned.1.call-update) | async-done | bytes 2097168 | tf_op jit(solution)/shard_map/cond/branch_1_fun/psum | solution.py:433
  222.4 7.9 %mix_experts.3 = (f32[4,64,1792]{2,1,0:T(8,128)S(1)}, bf16[256,1792]{1,0:T(8,128)(2,1)}) custom-call(f32[512,1024]{1,0:T(8,128)S(1)} %copy-done.52, s32[512,2]{1,0:T(8,128)S(1)} %copy-done.88, f32[512,2]{1,0:T(8,128)} %get-tuple-element.106.weights_ref, bf16[4,2,128,1792]{3,2,1,0:T(8,128)(2,1)} %get-tuple-element.107.down_ref, ...), custom_call_target="tpu_custom_call" | custom-call | flops 1 | bytes 1 | tf_op jit(solution)/shard_map/cond/branch_1_fun/mix_experts/pallas_call | solution.py:658
  242.5 11.7 %collective-permute-done.50.refs_4_.refs_0_.refs_2_.refs_1_.refs_3_ = bf16[3,4,1,32,1792]{4,3,2,1,0:T(8,128)(2,1)} collective-permute-done((bf16[3,4,1,32,1792]{4,3,2,1,0:T(8,128)(2,1)}, bf16[3,4,1,32,1792]{4,3,2,1,0:T(8,128)(2,1)}, u32[]{:S(2)}, u32[]{:S(2)}) %collective-permute-start.50) | collective-permute-done | bytes 1376288 | tf_op jit(solution)/shard_map/cond/branch_1_fun/ppermute | solution.py:514
  306.3 6.9 %collective-permute-done.57.refs_1_.refs_4_.refs_3_ = bf16[3,4,1,32,1792]{4,3,2,1,0:T(8,128)(2,1)S(1)} collective-permute-done((bf16[3,4,1,32,1792]{4,3,2,1,0:T(8,128)(2,1)}, bf16[3,4,1,32,1792]{4,3,2,1,0:T(8,128)(2,1)S(1)}, u32[]{:S(2)}, u32[]{:S(2)}) %collective-permute-start.57) | collective-permute-done | bytes 1376288 | tf_op jit(solution)/shard_map/cond/branch_1_fun/ppermute | solution.py:514
  322.8 5.2 %collective-permute-start.66 = (bf16[2,4,1,32,1792]{4,3,2,1,0:T(8,128)(2,1)}, bf16[2,4,1,32,1792]{4,3,2,1,0:T(8,128)(2,1)}, u32[]{:S(2)}, u32[]{:S(2)}) collective-permute-start(bf16[2,4,1,32,1792]{4,3,2,1,0:T(8,128)(2,1)} %pack.140.refs_1_), channel_id=1, source_target_pairs={{0,1},{2,3},{4,5},{6,7},{1,0},{3,2},{5,4},{7,6},{8,9},{10,11},{12,... | collective-permute-start | bytes 2752520 | tf_op jit(solution)/shard_map/cond/branch_1_fun/ppermute | solution.py:404
  336.1 6.5 %collective-permute-done.65.refs_1_.refs_3_.refs_4_.refs_2_ = bf16[3,4,1,32,1792]{4,3,2,1,0:T(8,128)(2,1)S(1)} collective-permute-done((bf16[3,4,1,32,1792]{4,3,2,1,0:T(8,128)(2,1)}, bf16[3,4,1,32,1792]{4,3,2,1,0:T(8,128)(2,1)S(1)}, u32[]{:S(2)}, u32[]{:S(2)}) %collective-permute-start.65) | collective-permute-done | bytes 1376288 | tf_op jit(solution)/shard_map/cond/branch_1_fun/ppermute | solution.py:514
  348.7 5.2 %collective-permute-start.72 = (bf16[3,4,1,32,1792]{4,3,2,1,0:T(8,128)(2,1)}, bf16[3,4,1,32,1792]{4,3,2,1,0:T(8,128)(2,1)}, u32[]{:S(2)}, u32[]{:S(2)}) collective-permute-start(bf16[3,4,1,32,1792]{4,3,2,1,0:T(8,128)(2,1)} %pack.143.refs_1_), channel_id=1, source_target_pairs={{0,1},{2,3},{4,5},{6,7},{1,0},{3,2},{5,4},{7,6},{8,9},{10,11},{12,... | collective-permute-start | bytes 4128776 | tf_op jit(solution)/shard_map/cond/branch_1_fun/ppermute | solution.py:404
  364.0 8.2 %collective-permute-done.64.refs_1_.refs_3_ = bf16[3,4,1,32,1792]{4,3,2,1,0:T(8,128)(2,1)} collective-permute-done((bf16[3,4,1,32,1792]{4,3,2,1,0:T(8,128)(2,1)}, bf16[3,4,1,32,1792]{4,3,2,1,0:T(8,128)(2,1)}, u32[]{:S(2)}, u32[]{:S(2)}) %collective-permute-start.64) | collective-permute-done | bytes 1376288 | tf_op jit(solution)/shard_map/cond/branch_1_fun/ppermute | solution.py:514
  380.3 6.1 %collective-permute-start.68 = (bf16[2,4,1,32,1792]{4,3,2,1,0:T(8,128)(2,1)}, bf16[2,4,1,32,1792]{4,3,2,1,0:T(8,128)(2,1)}, u32[]{:S(2)}, u32[]{:S(2)}) collective-permute-start(bf16[2,4,1,32,1792]{4,3,2,1,0:T(8,128)(2,1)} %pack.151.refs_6_), channel_id=1, source_target_pairs={{0,2},{2,0},{4,6},{6,4},{1,3},{3,1},{5,7},{7,5},{8,10},{10,8},{12,... | collective-permute-start | bytes 2752520 | tf_op jit(solution)/shard_map/cond/branch_1_fun/ppermute | solution.py:514
  393.5 19.1 %collective-permute-done.70.refs_0_ = bf16[4,4,1,32,1792]{4,3,2,1,0:T(8,128)(2,1)S(1)} collective-permute-done((bf16[4,4,1,32,1792]{4,3,2,1,0:T(8,128)(2,1)}, bf16[4,4,1,32,1792]{4,3,2,1,0:T(8,128)(2,1)S(1)}, u32[]{:S(2)}, u32[]{:S(2)}) %collective-permute-start.70) | collective-permute-done | bytes 1835040 | tf_op jit(solution)/shard_map/cond/branch_1_fun/ppermute | solution.py:488
  415.9 5.4 %collective-permute-start.69 = (bf16[1,4,1,32,1792]{4,3,2,1,0:T(8,128)(2,1)S(1)}, bf16[1,4,1,32,1792]{4,3,2,1,0:T(8,128)(2,1)S(1)}, u32[]{:S(2)}, u32[]{:S(2)}) collective-permute-start(bf16[1,4,1,32,1792]{4,3,2,1,0:T(8,128)(2,1)S(1)} %copy-done.64), channel_id=1, source_target_pairs={{0,1},{2,3},{4,5},{6,7},{1,0},{3,2},{5,4},{7,6},{8,9},{10,11},{12,... | collective-permute-start | bytes 1376264 | tf_op jit(solution)/shard_map/cond/branch_1_fun/ppermute | solution.py:404
  426.8 15.2 %collective-permute-done.77.refs_0_ = bf16[3,4,1,32,1792]{4,3,2,1,0:T(8,128)(2,1)} collective-permute-done((bf16[3,4,1,32,1792]{4,3,2,1,0:T(8,128)(2,1)}, bf16[3,4,1,32,1792]{4,3,2,1,0:T(8,128)(2,1)}, u32[]{:S(2)}, u32[]{:S(2)}) %collective-permute-start.77) | collective-permute-done | bytes 1376288 | tf_op jit(solution)/shard_map/cond/branch_1_fun/ppermute | solution.py:488
  (248 shorter events, 243.5 us)
Async XLA Ops:
  19.7 45.9 %all-to-all-start.4 = ((bf16[4,4,2,32,1792]{4,3,2,1,0:T(8,128)(2,1)}), bf16[4,4,2,32,1792]{4,3,2,1,0:T(8,128)(2,1)}, u32[]{:S(2)}, u32[]{:S(2)}) async-start(bf16[4,4,2,32,1792]{4,3,2,1,0:T(8,128)(2,1)} %copy-done.37), calls=%async_computation.4 | async-start | bytes 7340032 | tf_op jit(solution)/shard_map/all_to_all | solution.py:806
  65.6 45.3 %all-to-all-start.2 = ((bf16[4,4,2,32,1792]{4,3,2,1,0:T(8,128)(2,1)}), bf16[4,4,2,32,1792]{4,3,2,1,0:T(8,128)(2,1)}, u32[]{:S(2)}, u32[]{:S(2)}) async-start(bf16[4,4,2,32,1792]{4,3,2,1,0:T(8,128)(2,1)} %get-tuple-element.101), calls=%async_computation.2 | async-start | bytes 7340032 | tf_op jit(solution)/shard_map/cond/branch_1_fun/all_to_all | solution.py:342
  76.4 42.8 %collective-permute-start.43 = (bf16[3,4,1,32,1792]{4,3,2,1,0:T(8,128)(2,1)}, bf16[3,4,1,32,1792]{4,3,2,1,0:T(8,128)(2,1)S(1)}, u32[]{:S(2)}, u32[]{:S(2)}) collective-permute-start(bf16[3,4,1,32,1792]{4,3,2,1,0:T(8,128)(2,1)} %pack.120.refs_0_), channel_id=1, source_target_pairs={{0,2},{2,0},{4,6},{6,4},{1,3},{3,1},{5,7},{7,5},{8,10},{10,8},{12,... | collective-permute-start | bytes 4128776 | tf_op jit(solution)/shard_map/cond/branch_1_fun/ppermute | solution.py:514
  93.1 43.2 %collective-permute-start.41 = (bf16[3,4,1,32,1792]{4,3,2,1,0:T(8,128)(2,1)}, bf16[3,4,1,32,1792]{4,3,2,1,0:T(8,128)(2,1)}, u32[]{:S(2)}, u32[]{:S(2)}) collective-permute-start(bf16[3,4,1,32,1792]{4,3,2,1,0:T(8,128)(2,1)} %pack.122.refs_1_), channel_id=1, source_target_pairs={{0,2},{2,0},{4,6},{6,4},{1,3},{3,1},{5,7},{7,5},{8,10},{10,8},{12,... | collective-permute-start | bytes 4128776 | tf_op jit(solution)/shard_map/cond/branch_1_fun/ppermute | solution.py:514
  110.9 88.8 %all-to-all-start.3 = ((bf16[4,4,2,32,1792]{4,3,2,1,0:T(8,128)(2,1)}), bf16[4,4,2,32,1792]{4,3,2,1,0:T(8,128)(2,1)}, u32[]{:S(2)}, u32[]{:S(2)}) async-start(bf16[4,4,2,32,1792]{4,3,2,1,0:T(8,128)(2,1)} %get-tuple-element.102), calls=%async_computation.3 | async-start | bytes 7340032 | tf_op jit(solution)/shard_map/cond/branch_1_fun/all_to_all | solution.py:342
  116.7 104.0 %all-reduce.6.cloned.1.call-start = ((), (), s32[]{:S(2)}) async-start(), calls=%async_computation.6 | async-start | bytes 4194304 | tf_op jit(solution)/shard_map/cond/branch_1_fun/psum | solution.py:433
  125.8 42.6 %collective-permute-start.48 = (bf16[3,4,1,32,1792]{4,3,2,1,0:T(8,128)(2,1)}, bf16[3,4,1,32,1792]{4,3,2,1,0:T(8,128)(2,1)}, u32[]{:S(2)}, u32[]{:S(2)}) collective-permute-start(bf16[3,4,1,32,1792]{4,3,2,1,0:T(8,128)(2,1)} %pack.124.refs_2_), channel_id=1, source_target_pairs={{2,4},{4,2},{0,1},{6,7},{3,5},{5,3},{1,0},{7,6},{10,12},{12,10},{8... | collective-permute-start | bytes 4128776 | tf_op jit(solution)/shard_map/cond/branch_1_fun/ppermute | solution.py:488
  142.9 52.4 %collective-permute-start.46 = (bf16[3,4,1,32,1792]{4,3,2,1,0:T(8,128)(2,1)}, bf16[3,4,1,32,1792]{4,3,2,1,0:T(8,128)(2,1)S(1)}, u32[]{:S(2)}, u32[]{:S(2)}) collective-permute-start(bf16[3,4,1,32,1792]{4,3,2,1,0:T(8,128)(2,1)} %pack.127.refs_3_), channel_id=1, source_target_pairs={{0,2},{2,0},{4,6},{6,4},{1,3},{3,1},{5,7},{7,5},{8,10},{10,8},{12,... | collective-permute-start | bytes 4128776 | tf_op jit(solution)/shard_map/cond/branch_1_fun/ppermute | solution.py:514
  143.0 54.1 %collective-permute-start.45 = (bf16[3,4,1,32,1792]{4,3,2,1,0:T(8,128)(2,1)}, bf16[3,4,1,32,1792]{4,3,2,1,0:T(8,128)(2,1)}, u32[]{:S(2)}, u32[]{:S(2)}) collective-permute-start(bf16[3,4,1,32,1792]{4,3,2,1,0:T(8,128)(2,1)} %pack.126.refs_2_), channel_id=1, source_target_pairs={{2,4},{4,2},{0,1},{6,7},{3,5},{5,3},{1,0},{7,6},{10,12},{12,10},{8... | collective-permute-start | bytes 4128776 | tf_op jit(solution)/shard_map/cond/branch_1_fun/ppermute | solution.py:488
  173.9 57.6 %collective-permute-start.51 = (bf16[3,4,1,32,1792]{4,3,2,1,0:T(8,128)(2,1)}, bf16[3,4,1,32,1792]{4,3,2,1,0:T(8,128)(2,1)S(1)}, u32[]{:S(2)}, u32[]{:S(2)}) collective-permute-start(bf16[3,4,1,32,1792]{4,3,2,1,0:T(8,128)(2,1)} %pack.130.refs_2_), channel_id=1, source_target_pairs={{0,2},{2,0},{4,6},{6,4},{1,3},{3,1},{5,7},{7,5},{8,10},{10,8},{12,... | collective-permute-start | bytes 4128776 | tf_op jit(solution)/shard_map/cond/branch_1_fun/ppermute | solution.py:514
  175.3 59.2 %collective-permute-start.53 = (bf16[3,4,1,32,1792]{4,3,2,1,0:T(8,128)(2,1)}, bf16[3,4,1,32,1792]{4,3,2,1,0:T(8,128)(2,1)}, u32[]{:S(2)}, u32[]{:S(2)}) collective-permute-start(bf16[3,4,1,32,1792]{4,3,2,1,0:T(8,128)(2,1)} %pack.129.refs_3_), channel_id=1, source_target_pairs={{2,4},{4,2},{0,1},{6,7},{3,5},{5,3},{1,0},{7,6},{10,12},{12,10},{8... | collective-permute-start | bytes 4128776 | tf_op jit(solution)/shard_map/cond/branch_1_fun/ppermute | solution.py:488
  175.3 65.5 %collective-permute-start.52 = (bf16[3,4,1,32,1792]{4,3,2,1,0:T(8,128)(2,1)}, bf16[3,4,1,32,1792]{4,3,2,1,0:T(8,128)(2,1)}, u32[]{:S(2)}, u32[]{:S(2)}) collective-permute-start(bf16[3,4,1,32,1792]{4,3,2,1,0:T(8,128)(2,1)} %pack.128.refs_1_), channel_id=1, source_target_pairs={{0,1},{2,3},{4,5},{6,7},{1,0},{3,2},{5,4},{7,6},{8,9},{10,11},{12,... | collective-permute-start | bytes 4128776 | tf_op jit(solution)/shard_map/cond/branch_1_fun/ppermute | solution.py:404
  202.6 51.6 %collective-permute-start.50 = (bf16[3,4,1,32,1792]{4,3,2,1,0:T(8,128)(2,1)}, bf16[3,4,1,32,1792]{4,3,2,1,0:T(8,128)(2,1)}, u32[]{:S(2)}, u32[]{:S(2)}) collective-permute-start(bf16[3,4,1,32,1792]{4,3,2,1,0:T(8,128)(2,1)} %pack.133.refs_0_), channel_id=1, source_target_pairs={{0,2},{2,0},{4,6},{6,4},{1,3},{3,1},{5,7},{7,5},{8,10},{10,8},{12,... | collective-permute-start | bytes 4128776 | tf_op jit(solution)/shard_map/cond/branch_1_fun/ppermute | solution.py:514
  203.0 56.2 %collective-permute-start.55 = (bf16[3,4,1,32,1792]{4,3,2,1,0:T(8,128)(2,1)}, bf16[3,4,1,32,1792]{4,3,2,1,0:T(8,128)(2,1)}, u32[]{:S(2)}, u32[]{:S(2)}) collective-permute-start(bf16[3,4,1,32,1792]{4,3,2,1,0:T(8,128)(2,1)} %pack.132.refs_3_), channel_id=1, source_target_pairs={{2,4},{4,2},{0,1},{6,7},{3,5},{5,3},{1,0},{7,6},{10,12},{12,10},{8... | collective-permute-start | bytes 4128776 | tf_op jit(solution)/shard_map/cond/branch_1_fun/ppermute | solution.py:488
  240.2 43.4 %collective-permute-start.58 = (bf16[3,4,1,32,1792]{4,3,2,1,0:T(8,128)(2,1)}, bf16[3,4,1,32,1792]{4,3,2,1,0:T(8,128)(2,1)S(1)}, u32[]{:S(2)}, u32[]{:S(2)}) collective-permute-start(bf16[3,4,1,32,1792]{4,3,2,1,0:T(8,128)(2,1)} %pack.136.refs_3_), channel_id=1, source_target_pairs={{0,2},{2,0},{4,6},{6,4},{1,3},{3,1},{5,7},{7,5},{8,10},{10,8},{12,... | collective-permute-start | bytes 4128776 | tf_op jit(solution)/shard_map/cond/branch_1_fun/ppermute | solution.py:514
  240.9 52.8 %collective-permute-start.60 = (bf16[3,4,1,32,1792]{4,3,2,1,0:T(8,128)(2,1)}, bf16[3,4,1,32,1792]{4,3,2,1,0:T(8,128)(2,1)S(1)}, u32[]{:S(2)}, u32[]{:S(2)}) collective-permute-start(bf16[3,4,1,32,1792]{4,3,2,1,0:T(8,128)(2,1)} %pack.135.refs_2_), channel_id=1, source_target_pairs={{2,4},{4,2},{0,1},{6,7},{3,5},{5,3},{1,0},{7,6},{10,12},{12,10},{8... | collective-permute-start | bytes 4128776 | tf_op jit(solution)/shard_map/cond/branch_1_fun/ppermute | solution.py:488
  240.9 59.6 %collective-permute-start.59 = (bf16[3,4,1,32,1792]{4,3,2,1,0:T(8,128)(2,1)}, bf16[3,4,1,32,1792]{4,3,2,1,0:T(8,128)(2,1)}, u32[]{:S(2)}, u32[]{:S(2)}) collective-permute-start(bf16[3,4,1,32,1792]{4,3,2,1,0:T(8,128)(2,1)} %pack.134.refs_1_), channel_id=1, source_target_pairs={{0,1},{2,3},{4,5},{6,7},{1,0},{3,2},{5,4},{7,6},{8,9},{10,11},{12,... | collective-permute-start | bytes 4128776 | tf_op jit(solution)/shard_map/cond/branch_1_fun/ppermute | solution.py:404
  299.5 43.1 %collective-permute-start.65 = (bf16[3,4,1,32,1792]{4,3,2,1,0:T(8,128)(2,1)}, bf16[3,4,1,32,1792]{4,3,2,1,0:T(8,128)(2,1)S(1)}, u32[]{:S(2)}, u32[]{:S(2)}) collective-permute-start(bf16[3,4,1,32,1792]{4,3,2,1,0:T(8,128)(2,1)} %pack.142.refs_4_), channel_id=1, source_target_pairs={{0,2},{2,0},{4,6},{6,4},{1,3},{3,1},{5,7},{7,5},{8,10},{10,8},{12,... | collective-permute-start | bytes 4128776 | tf_op jit(solution)/shard_map/cond/branch_1_fun/ppermute | solution.py:514
  300.4 44.1 %collective-permute-start.67 = (bf16[3,4,1,32,1792]{4,3,2,1,0:T(8,128)(2,1)}, bf16[3,4,1,32,1792]{4,3,2,1,0:T(8,128)(2,1)S(1)}, u32[]{:S(2)}, u32[]{:S(2)}) collective-permute-start(bf16[3,4,1,32,1792]{4,3,2,1,0:T(8,128)(2,1)} %pack.141.refs_4_), channel_id=1, source_target_pairs={{2,4},{4,2},{0,1},{6,7},{3,5},{5,3},{1,0},{7,6},{10,12},{12,10},{8... | collective-permute-start | bytes 4128776 | tf_op jit(solution)/shard_map/cond/branch_1_fun/ppermute | solution.py:488
  321.9 50.3 %collective-permute-start.64 = (bf16[3,4,1,32,1792]{4,3,2,1,0:T(8,128)(2,1)}, bf16[3,4,1,32,1792]{4,3,2,1,0:T(8,128)(2,1)}, u32[]{:S(2)}, u32[]{:S(2)}) collective-permute-start(bf16[3,4,1,32,1792]{4,3,2,1,0:T(8,128)(2,1)} %pack.145.refs_3_), channel_id=1, source_target_pairs={{0,2},{2,0},{4,6},{6,4},{1,3},{3,1},{5,7},{7,5},{8,10},{10,8},{12,... | collective-permute-start | bytes 4128776 | tf_op jit(solution)/shard_map/cond/branch_1_fun/ppermute | solution.py:514
  322.8 52.0 %collective-permute-start.63 = (bf16[3,4,1,32,1792]{4,3,2,1,0:T(8,128)(2,1)}, bf16[3,4,1,32,1792]{4,3,2,1,0:T(8,128)(2,1)}, u32[]{:S(2)}, u32[]{:S(2)}) collective-permute-start(bf16[3,4,1,32,1792]{4,3,2,1,0:T(8,128)(2,1)} %pack.144.refs_3_), channel_id=1, source_target_pairs={{2,4},{4,2},{0,1},{6,7},{3,5},{5,3},{1,0},{7,6},{10,12},{12,10},{8... | collective-permute-start | bytes 4128776 | tf_op jit(solution)/shard_map/cond/branch_1_fun/ppermute | solution.py:488
  348.5 64.0 %collective-permute-start.70 = (bf16[4,4,1,32,1792]{4,3,2,1,0:T(8,128)(2,1)}, bf16[4,4,1,32,1792]{4,3,2,1,0:T(8,128)(2,1)S(1)}, u32[]{:S(2)}, u32[]{:S(2)}) collective-permute-start(bf16[4,4,1,32,1792]{4,3,2,1,0:T(8,128)(2,1)} %pack.147.refs_2_), channel_id=1, source_target_pairs={{2,4},{4,2},{0,1},{6,7},{3,5},{5,3},{1,0},{7,6},{10,12},{12,10},{8... | collective-permute-start | bytes 5505032 | tf_op jit(solution)/shard_map/cond/branch_1_fun/ppermute | solution.py:488
  377.6 64.5 %collective-permute-start.77 = (bf16[3,4,1,32,1792]{4,3,2,1,0:T(8,128)(2,1)}, bf16[3,4,1,32,1792]{4,3,2,1,0:T(8,128)(2,1)}, u32[]{:S(2)}, u32[]{:S(2)}) collective-permute-start(bf16[3,4,1,32,1792]{4,3,2,1,0:T(8,128)(2,1)} %pack.150.refs_2_), channel_id=1, source_target_pairs={{2,4},{4,2},{0,1},{6,7},{3,5},{5,3},{1,0},{7,6},{10,12},{12,10},{8... | collective-permute-start | bytes 4128776 | tf_op jit(solution)/shard_map/cond/branch_1_fun/ppermute | solution.py:488
  380.3 44.6 %collective-permute-start.68 = (bf16[2,4,1,32,1792]{4,3,2,1,0:T(8,128)(2,1)}, bf16[2,4,1,32,1792]{4,3,2,1,0:T(8,128)(2,1)}, u32[]{:S(2)}, u32[]{:S(2)}) collective-permute-start(bf16[2,4,1,32,1792]{4,3,2,1,0:T(8,128)(2,1)} %pack.151.refs_6_), channel_id=1, source_target_pairs={{0,2},{2,0},{4,6},{6,4},{1,3},{3,1},{5,7},{7,5},{8,10},{10,8},{12,... | collective-permute-start | bytes 2752520 | tf_op jit(solution)/shard_map/cond/branch_1_fun/ppermute | solution.py:514
  (67 other events, 950.7 us)
Sparse Core Ops, SparseCore 0:
  10.2 29.0 all-gather.1
  148.7 72.0 all-reduce.5
where the time goes:
time: 490 us; the launch traced here: 486 us
  Pallas kernels  204 us (42%)
  waiting for transfers between devices  163 us (33%)
  starting transfers between devices  80.4 us (16%)
  local copies, waits for them, and re-layouts  18.4 us (4%)
  between operations  14.7 us (3%)
    pallas_call x39, Pallas kernels, pack(): pl.pallas_call(functools.partial(pack_kernel, pieces, n_in), in_specs=[sm...  98.7 us
    ppermute x14, waiting for transfers between devices, line_exchange(): got_edge[n] = lax.ppermute(packed(pieces, after), 'roll', edge_pairs)  77.7 us
    pallas_call x22, Pallas kernels, place_pieces(): pl.pallas_call(functools.partial(place_kernel, pieces, sources, first, bl...  57.8 us
    ppermute x13, starting transfers between devices, swap(): lax.ppermute(packed([find(c, p, 'mate') for _, c, p in taken]), 'roll', s...  41.8 us
    ppermute x12, waiting for transfers between devices, line_exchange(): got_middle[n] = lax.ppermute(packed(pieces, after), 'roll', middle_pairs)  35.3 us
    pallas_call x3, Pallas kernels, quantize(): pl.pallas_call(functools.partial(quantize_kernel, trains), grid=(experts,...  26.3 us
    psum x1, waiting for transfers between devices, ride_first(): ride['pre'] = lax.psum(pre, 'train')  17.8 us
    ppermute x14, starting transfers between devices, line_exchange(): got_edge[n] = lax.ppermute(packed(pieces, after), 'roll', edge_pairs)  16.8 us
  transfers between devices with their start and end apart: 45, of which 16 were waited for; matrix products, arithmetic and copies ran while one was open for 1% of the time, Pallas kernels for 41%

commit v1 on v0

--- a/solution.py
+++ b/solution.py
@@ -275,7 +275,7 @@
             c = own.pop(0)
             across = [("own", c, s) for s in range(cap)]
         if across:
-            relayed += [(n + 2, (across[0][0], c, i)) for i in range(CORES)]
+            relayed += [(n + (2 if n else 1), (across[0][0], c, i)) for i in range(CORES)]
         if ride_due.get("across", n + 1) <= n and (not across or across[0][0] == "own"):
             across.append(("ride", 0, 0))
             del ride_due["across"]
@@ -325,7 +325,7 @@
     shape = (trains, 1, rows, features)
     chunks = [(m, b) for m in range(3) for b in range(blocks)]
     count = len(chunks)
-    opens = [(0, 2, 5)[m] for m, _ in chunks]
+    opens = [(0, 2, 5 if cap < experts else 4)[m] for m, _ in chunks]
     ride_from = 8
     middle, inwards, outwards = line_schedule(opens, experts, cap, ride_from)
     rounds = len(outwards)

time: 490 us -> 487 us (level)
  starting transfers between devices: 80.4 us -> 69.4 us
  waiting for transfers between devices: 163 us -> 172 us
    ppermute x12, waiting for transfers between devices: 35.3 us -> 59.3 us  [line_exchange(): got_middle[n] = lax.ppermute(packed(pieces, after), 'roll', middle_pairs)]
    all_to_all x2, waiting for transfers between devices: 15.4 us -> 4.07 us  [line_exchange(): lax.all_to_all(quant, 'train', split_axis=0, concat_axis=0, tiled=True)]
    ppermute x13 -> x14, starting transfers between devices: 41.8 us -> 31.7 us  [swap(): lax.ppermute(packed([find(c, p, 'mate') for _, c, p in taken]), 'roll', s...]
    psum x1, waiting for transfers between devices: 17.8 us -> 11 us  [ride_first(): ride['pre'] = lax.psum(pre, 'train')]
    cond x87 -> x83, local copies, waits for them, and re-layouts: 11.8 us -> 9.79 us
    pallas_call x39 -> x40, Pallas kernels: 98.7 us -> 99.7 us  [pack(): pl.pallas_call(functools.partial(pack_kernel, pieces, n_in), in_specs=[sm...]
  transfers between devices with their start and end apart: 45 -> 46, of which waited for: 16 -> 18; matrix products, arithmetic and copies ran while one was open for 1% -> 1% of each run, Pallas kernels for 41% -> 42%
where the time goes in v1:
time: 487 us; the launch traced here: 483 us
  Pallas kernels  206 us (42%)
  waiting for transfers between devices  172 us (35%)
  starting transfers between devices  69.4 us (14%)
  local copies, waits for them, and re-layouts  16.4 us (3%)
  between operations  14.7 us (3%)
    pallas_call x40, Pallas kernels, pack(): pl.pallas_call(functools.partial(pack_kernel, pieces, n_in), in_specs=[sm...  99.7 us
    ppermute x14, waiting for transfers between devices, line_exchange(): got_edge[n] = lax.ppermute(packed(pieces, after), 'roll', edge_pairs)  80.7 us
    pallas_call x22, Pallas kernels, place_pieces(): pl.pallas_call(functools.partial(place_kernel, pieces, sources, first, bl...  59.7 us
    ppermute x12, waiting for transfers between devices, line_exchange(): got_middle[n] = lax.ppermute(packed(pieces, after), 'roll', middle_pairs)  59.3 us
    ppermute x14, starting transfers between devices, swap(): lax.ppermute(packed([find(c, p, 'mate') for _, c, p in taken]), 'roll', s...  31.7 us
    pallas_call x3, Pallas kernels, quantize(): pl.pallas_call(functools.partial(quantize_kernel, trains), grid=(experts,...  26.3 us
    ppermute x14, starting transfers between devices, line_exchange(): got_edge[n] = lax.ppermute(packed(pieces, after), 'roll', edge_pairs)  16.1 us
    all_to_all x1, waiting for transfers between devices, per_device(): lax.all_to_all(quant, 'train', split_axis=0, concat_axis=0, tiled=True)  15.5 us
  transfers between devices with their start and end apart: 46, of which 18 were waited for; matrix products, arithmetic and copies ran while one was open for 1% of the time, Pallas kernels for 42%

profile of v1, /device:TPU:19, one launch (start us, length us, event | category | flops | bytes accessed | tf_op | source)
XLA Modules:
  0.0 483.4 jit_solution(10699150578179167267)
XLA Ops:
  9.6 8.3 %quantize.3 = (bf16[4,4,2,32,1792]{4,3,2,1,0:T(8,128)(2,1)S(1)}, bf16[4,2,128,1792]{3,2,1,0:T(8,128)(2,1)}) custom-call(f32[4,256,1792]{2,1,0:T(8,128)} %x_ref.3), custom_call_target="tpu_custom_call" | custom-call | flops 1 | bytes 1 | tf_op jit(solution)/shard_map/quantize/pallas_call | solution.py:42
  19.7 5.0 %all-to-all-start.4 = ((bf16[4,4,2,32,1792]{4,3,2,1,0:T(8,128)(2,1)}), bf16[4,4,2,32,1792]{4,3,2,1,0:T(8,128)(2,1)}, u32[]{:S(2)}, u32[]{:S(2)}) async-start(bf16[4,4,2,32,1792]{4,3,2,1,0:T(8,128)(2,1)} %copy-done.30), calls=%async_computation.4 | async-start | bytes 7340032 | tf_op jit(solution)/shard_map/all_to_all | solution.py:806
  26.0 8.3 %quantize.4 = (bf16[4,4,2,32,1792]{4,3,2,1,0:T(8,128)(2,1)S(1)}, bf16[4,2,128,1792]{3,2,1,0:T(8,128)(2,1)}) custom-call(f32[4,256,1792]{2,1,0:T(8,128)} %x_ref.4, s32[29]{0:T(128)S(1)} %plan.1.refs_0_), custom_call_target="tpu_custom_call" | custom-call | flops 1 | bytes 1 | tf_op jit(solution)/shard_map/quantize/pallas_call | solution.py:42
  34.3 9.7 %quantize.5 = (bf16[4,4,2,32,1792]{4,3,2,1,0:T(8,128)(2,1)}, bf16[4,2,128,1792]{3,2,1,0:T(8,128)(2,1)}) custom-call(f32[4,256,1792]{2,1,0:T(8,128)} %x_ref.5, bf16[4,4,2,32,1792]{4,3,2,1,0:T(8,128)(2,1)S(1)} %get-tuple-element.175.refs_0_), custom_call_target="tpu_custom_call" | custom-call | flops 1 | bytes 1 | tf_op jit(solution)/shard_map/quantize/pallas_call | solution.py:42
  50.1 15.5 %all-to-all-done.4 = bf16[4,4,2,32,1792]{4,3,2,1,0:T(8,128)(2,1)} async-done(((bf16[4,4,2,32,1792]{4,3,2,1,0:T(8,128)(2,1)}), bf16[4,4,2,32,1792]{4,3,2,1,0:T(8,128)(2,1)}, u32[]{:S(2)}, u32[]{:S(2)}) %all-to-all-start.4) | async-done | bytes 3670048 | tf_op jit(solution)/shard_map/all_to_all | solution.py:806
  65.6 409.8 %conditional.1 = (bf16[16,32,7168]{2,1,0:T(8,128)(2,1)}, bf16[16,32,7168]{2,1,0:T(8,128)(2,1)}, bf16[16,32,7168]{2,1,0:T(8,128)(2,1)}, bf16[64,1792]{1,0:T(8,128)(2,1)}) conditional(s32[]{:T(128)} %bitcast.17, (s32[29]{0:T(128)S(1)}, bf16[4,4,2,32,1792]{4,3,2,1,0:T(8,128)(2,1)}, bf16[512,1792]{1,0:T(8,128)(2,1)}, s32[512,2]{1,0:T(8,128)S(1)}, ...), branch_computations={%region_0.2_spmd, %region_2.4_spmd} | conditional | flops 524359 | bytes 473172832 | solution.py:819
  65.6 5.2 %all-to-all-start.2 = ((bf16[4,4,2,32,1792]{4,3,2,1,0:T(8,128)(2,1)}), bf16[4,4,2,32,1792]{4,3,2,1,0:T(8,128)(2,1)}, u32[]{:S(2)}, u32[]{:S(2)}) async-start(bf16[4,4,2,32,1792]{4,3,2,1,0:T(8,128)(2,1)} %get-tuple-element.103), calls=%async_computation.2 | async-start | bytes 7340032 | tf_op jit(solution)/shard_map/cond/branch_1_fun/all_to_all | solution.py:342
  91.8 12.0 %collective-permute-done.41.refs_0_.refs_2_ = bf16[3,4,1,32,1792]{4,3,2,1,0:T(8,128)(2,1)} collective-permute-done((bf16[3,4,1,32,1792]{4,3,2,1,0:T(8,128)(2,1)}, bf16[3,4,1,32,1792]{4,3,2,1,0:T(8,128)(2,1)}, u32[]{:S(2)}, u32[]{:S(2)}) %collective-permute-start.41) | collective-permute-done | bytes 1376288 | tf_op jit(solution)/shard_map/cond/branch_1_fun/ppermute | solution.py:488
  110.9 5.9 %all-to-all-start.3 = ((bf16[4,4,2,32,1792]{4,3,2,1,0:T(8,128)(2,1)}), bf16[4,4,2,32,1792]{4,3,2,1,0:T(8,128)(2,1)}, u32[]{:S(2)}, u32[]{:S(2)}) async-start(bf16[4,4,2,32,1792]{4,3,2,1,0:T(8,128)(2,1)} %get-tuple-element.104), calls=%async_computation.3 | async-start | bytes 7340032 | tf_op jit(solution)/shard_map/cond/branch_1_fun/all_to_all | solution.py:342
  127.8 10.6 %collective-permute-done.42.refs_1_.refs_0_.refs_3_ = bf16[3,4,1,32,1792]{4,3,2,1,0:T(8,128)(2,1)S(1)} collective-permute-done((bf16[3,4,1,32,1792]{4,3,2,1,0:T(8,128)(2,1)}, bf16[3,4,1,32,1792]{4,3,2,1,0:T(8,128)(2,1)S(1)}, u32[]{:S(2)}, u32[]{:S(2)}) %collective-permute-start.42) | collective-permute-done | bytes 1376288 | tf_op jit(solution)/shard_map/cond/branch_1_fun/ppermute | solution.py:514
  152.7 12.7 %collective-permute-done.48.refs_2_.refs_0_ = bf16[3,4,1,32,1792]{4,3,2,1,0:T(8,128)(2,1)} collective-permute-done((bf16[3,4,1,32,1792]{4,3,2,1,0:T(8,128)(2,1)}, bf16[3,4,1,32,1792]{4,3,2,1,0:T(8,128)(2,1)}, u32[]{:S(2)}, u32[]{:S(2)}) %collective-permute-start.48) | collective-permute-done | bytes 1376288 | tf_op jit(solution)/shard_map/cond/branch_1_fun/ppermute | solution.py:488
  183.4 14.0 %collective-permute-done.46.refs_1_.refs_0_.refs_3_ = bf16[3,4,1,32,1792]{4,3,2,1,0:T(8,128)(2,1)S(1)} collective-permute-done((bf16[3,4,1,32,1792]{4,3,2,1,0:T(8,128)(2,1)}, bf16[3,4,1,32,1792]{4,3,2,1,0:T(8,128)(2,1)S(1)}, u32[]{:S(2)}, u32[]{:S(2)}) %collective-permute-start.46) | collective-permute-done | bytes 1376288 | tf_op jit(solution)/shard_map/cond/branch_1_fun/ppermute | solution.py:514
  209.8 11.0 %all-reduce.6.cloned.1.call-done.pre_ref = f32[512,1024]{1,0:T(8,128)} async-done(((f32[512,1024]{1,0:T(8,128)}), f32[512,1024]{1,0:T(8,128)}) %all-reduce.6.cloned.1.call-update) | async-done | bytes 2097168 | tf_op jit(solution)/shard_map/cond/branch_1_fun/psum | solution.py:433
  222.4 7.8 %mix_experts.3 = (f32[4,64,1792]{2,1,0:T(8,128)S(1)}, bf16[256,1792]{1,0:T(8,128)(2,1)}) custom-call(f32[512,1024]{1,0:T(8,128)S(1)} %copy-done.48, s32[512,2]{1,0:T(8,128)S(1)} %copy-done.88, f32[512,2]{1,0:T(8,128)} %get-tuple-element.108.weights_ref, bf16[4,2,128,1792]{3,2,1,0:T(8,128)(2,1)} %get-tuple-element.109.down_ref, ...), custom_call_target="tpu_custom_call" | custom-call | flops 1 | bytes 1 | tf_op jit(solution)/shard_map/cond/branch_1_fun/mix_experts/pallas_call | solution.py:658
  243.9 12.5 %collective-permute-done.50.refs_3_.refs_0_.refs_4_.refs_1_ = bf16[3,4,1,32,1792]{4,3,2,1,0:T(8,128)(2,1)S(1)} collective-permute-done((bf16[3,4,1,32,1792]{4,3,2,1,0:T(8,128)(2,1)}, bf16[3,4,1,32,1792]{4,3,2,1,0:T(8,128)(2,1)S(1)}, u32[]{:S(2)}, u32[]{:S(2)}) %collective-permute-start.50) | collective-permute-done | bytes 1376288 | tf_op jit(solution)/shard_map/cond/branch_1_fun/ppermute | solution.py:514
  280.7 5.0 %collective-permute-done.59.refs_2_.refs_0_.refs_5_.refs_1_ = bf16[3,4,1,32,1792]{4,3,2,1,0:T(8,128)(2,1)S(1)} collective-permute-done((bf16[3,4,1,32,1792]{4,3,2,1,0:T(8,128)(2,1)S(1)}, bf16[3,4,1,32,1792]{4,3,2,1,0:T(8,128)(2,1)S(1)}, u32[]{:S(2)}, u32[]{:S(2)}) %collective-permute-start.59) | collective-permute-done | bytes 1376288 | tf_op jit(solution)/shard_map/cond/branch_1_fun/ppermute | solution.py:514
  285.7 4.3 collective-permute-start.55
  304.9 10.4 %collective-permute-done.58.refs_1_.refs_3_ = bf16[3,4,1,32,1792]{4,3,2,1,0:T(8,128)(2,1)S(1)} collective-permute-done((bf16[3,4,1,32,1792]{4,3,2,1,0:T(8,128)(2,1)}, bf16[3,4,1,32,1792]{4,3,2,1,0:T(8,128)(2,1)S(1)}, u32[]{:S(2)}, u32[]{:S(2)}) %collective-permute-start.58) | collective-permute-done | bytes 1376288 | tf_op jit(solution)/shard_map/cond/branch_1_fun/ppermute | solution.py:514
  321.0 4.6 collective-permute-start.66
  335.9 8.9 %collective-permute-done.68.refs_1_.refs_3_.refs_2_ = bf16[3,4,1,32,1792]{4,3,2,1,0:T(8,128)(2,1)S(1)} collective-permute-done((bf16[3,4,1,32,1792]{4,3,2,1,0:T(8,128)(2,1)}, bf16[3,4,1,32,1792]{4,3,2,1,0:T(8,128)(2,1)S(1)}, u32[]{:S(2)}, u32[]{:S(2)}) %collective-permute-start.68) | collective-permute-done | bytes 1376288 | tf_op jit(solution)/shard_map/cond/branch_1_fun/ppermute | solution.py:514
  362.8 11.1 %collective-permute-done.65.refs_1_.refs_3_ = bf16[2,4,1,32,1792]{4,3,2,1,0:T(8,128)(2,1)S(1)} collective-permute-done((bf16[2,4,1,32,1792]{4,3,2,1,0:T(8,128)(2,1)}, bf16[2,4,1,32,1792]{4,3,2,1,0:T(8,128)(2,1)S(1)}, u32[]{:S(2)}, u32[]{:S(2)}) %collective-permute-start.65) | collective-permute-done | bytes 917536 | tf_op jit(solution)/shard_map/cond/branch_1_fun/ppermute | solution.py:514
  395.4 15.8 %collective-permute-done.71.refs_0_ = bf16[4,4,1,32,1792]{4,3,2,1,0:T(8,128)(2,1)S(1)} collective-permute-done((bf16[4,4,1,32,1792]{4,3,2,1,0:T(8,128)(2,1)}, bf16[4,4,1,32,1792]{4,3,2,1,0:T(8,128)(2,1)S(1)}, u32[]{:S(2)}, u32[]{:S(2)}) %collective-permute-start.71) | collective-permute-done | bytes 1835040 | tf_op jit(solution)/shard_map/cond/branch_1_fun/ppermute | solution.py:488
  422.0 18.7 %collective-permute-done.78.refs_0_ = bf16[3,4,1,32,1792]{4,3,2,1,0:T(8,128)(2,1)} collective-permute-done((bf16[3,4,1,32,1792]{4,3,2,1,0:T(8,128)(2,1)}, bf16[3,4,1,32,1792]{4,3,2,1,0:T(8,128)(2,1)}, u32[]{:S(2)}, u32[]{:S(2)}) %collective-permute-start.78) | collective-permute-done | bytes 1376288 | tf_op jit(solution)/shard_map/cond/branch_1_fun/ppermute | solution.py:488
  457.4 5.5 %collective-permute-done.79.refs_1_ = bf16[2,4,1,32,1792]{4,3,2,1,0:T(8,128)(2,1)S(1)} collective-permute-done((bf16[2,4,1,32,1792]{4,3,2,1,0:T(8,128)(2,1)S(1)}, bf16[2,4,1,32,1792]{4,3,2,1,0:T(8,128)(2,1)S(1)}, u32[]{:S(2)}, u32[]{:S(2)}) %collective-permute-start.79) | collective-permute-done | bytes 917536 | tf_op jit(solution)/shard_map/cond/branch_1_fun/ppermute | solution.py:514
  (247 shorter events, 244.3 us)
Async XLA Ops:
  19.7 45.9 %all-to-all-start.4 = ((bf16[4,4,2,32,1792]{4,3,2,1,0:T(8,128)(2,1)}), bf16[4,4,2,32,1792]{4,3,2,1,0:T(8,128)(2,1)}, u32[]{:S(2)}, u32[]{:S(2)}) async-start(bf16[4,4,2,32,1792]{4,3,2,1,0:T(8,128)(2,1)} %copy-done.30), calls=%async_computation.4 | async-start | bytes 7340032 | tf_op jit(solution)/shard_map/all_to_all | solution.py:806
  65.6 45.3 %all-to-all-start.2 = ((bf16[4,4,2,32,1792]{4,3,2,1,0:T(8,128)(2,1)}), bf16[4,4,2,32,1792]{4,3,2,1,0:T(8,128)(2,1)}, u32[]{:S(2)}, u32[]{:S(2)}) async-start(bf16[4,4,2,32,1792]{4,3,2,1,0:T(8,128)(2,1)} %get-tuple-element.103), calls=%async_computation.2 | async-start | bytes 7340032 | tf_op jit(solution)/shard_map/cond/branch_1_fun/all_to_all | solution.py:342
  76.8 42.6 %collective-permute-start.43 = (bf16[3,4,1,32,1792]{4,3,2,1,0:T(8,128)(2,1)}, bf16[3,4,1,32,1792]{4,3,2,1,0:T(8,128)(2,1)S(1)}, u32[]{:S(2)}, u32[]{:S(2)}) collective-permute-start(bf16[3,4,1,32,1792]{4,3,2,1,0:T(8,128)(2,1)} %pack.121.refs_0_), channel_id=1, source_target_pairs={{0,2},{2,0},{4,6},{6,4},{1,3},{3,1},{5,7},{7,5},{8,10},{10,8},{12,... | collective-permute-start | bytes 4128776 | tf_op jit(solution)/shard_map/cond/branch_1_fun/ppermute | solution.py:514
  110.9 91.6 %all-to-all-start.3 = ((bf16[4,4,2,32,1792]{4,3,2,1,0:T(8,128)(2,1)}), bf16[4,4,2,32,1792]{4,3,2,1,0:T(8,128)(2,1)}, u32[]{:S(2)}, u32[]{:S(2)}) async-start(bf16[4,4,2,32,1792]{4,3,2,1,0:T(8,128)(2,1)} %get-tuple-element.104), calls=%async_computation.3 | async-start | bytes 7340032 | tf_op jit(solution)/shard_map/cond/branch_1_fun/all_to_all | solution.py:342
  116.8 104.0 %all-reduce.6.cloned.1.call-start = ((), (), s32[]{:S(2)}) async-start(), calls=%async_computation.6 | async-start | bytes 4194304 | tf_op jit(solution)/shard_map/cond/branch_1_fun/psum | solution.py:433
  121.9 43.6 %collective-permute-start.48 = (bf16[3,4,1,32,1792]{4,3,2,1,0:T(8,128)(2,1)}, bf16[3,4,1,32,1792]{4,3,2,1,0:T(8,128)(2,1)}, u32[]{:S(2)}, u32[]{:S(2)}) collective-permute-start(bf16[3,4,1,32,1792]{4,3,2,1,0:T(8,128)(2,1)} %pack.125.refs_1_), channel_id=1, source_target_pairs={{2,4},{4,2},{0,1},{6,7},{3,5},{5,3},{1,0},{7,6},{10,12},{12,10},{8... | collective-permute-start | bytes 4128776 | tf_op jit(solution)/shard_map/cond/branch_1_fun/ppermute | solution.py:488
  124.8 43.1 %collective-permute-start.49 = (bf16[3,4,1,32,1792]{4,3,2,1,0:T(8,128)(2,1)}, bf16[3,4,1,32,1792]{4,3,2,1,0:T(8,128)(2,1)}, u32[]{:S(2)}, u32[]{:S(2)}) collective-permute-start(bf16[3,4,1,32,1792]{4,3,2,1,0:T(8,128)(2,1)} %pack.126.refs_2_), channel_id=1, source_target_pairs={{0,2},{2,0},{4,6},{6,4},{1,3},{3,1},{5,7},{7,5},{8,10},{10,8},{12,... | collective-permute-start | bytes 4128776 | tf_op jit(solution)/shard_map/cond/branch_1_fun/ppermute | solution.py:514
  145.4 52.0 %collective-permute-start.46 = (bf16[3,4,1,32,1792]{4,3,2,1,0:T(8,128)(2,1)}, bf16[3,4,1,32,1792]{4,3,2,1,0:T(8,128)(2,1)S(1)}, u32[]{:S(2)}, u32[]{:S(2)}) collective-permute-start(bf16[3,4,1,32,1792]{4,3,2,1,0:T(8,128)(2,1)} %pack.129.refs_1_), channel_id=1, source_target_pairs={{0,2},{2,0},{4,6},{6,4},{1,3},{3,1},{5,7},{7,5},{8,10},{10,8},{12,... | collective-permute-start | bytes 4128776 | tf_op jit(solution)/shard_map/cond/branch_1_fun/ppermute | solution.py:514
  146.9 52.3 %collective-permute-start.45 = (bf16[3,4,1,32,1792]{4,3,2,1,0:T(8,128)(2,1)}, bf16[3,4,1,32,1792]{4,3,2,1,0:T(8,128)(2,1)}, u32[]{:S(2)}, u32[]{:S(2)}) collective-permute-start(bf16[3,4,1,32,1792]{4,3,2,1,0:T(8,128)(2,1)} %pack.128.refs_2_), channel_id=1, source_target_pairs={{2,4},{4,2},{0,1},{6,7},{3,5},{5,3},{1,0},{7,6},{10,12},{12,10},{8... | collective-permute-start | bytes 4128776 | tf_op jit(solution)/shard_map/cond/branch_1_fun/ppermute | solution.py:488
  173.3 60.0 %collective-permute-start.51 = (bf16[3,4,1,32,1792]{4,3,2,1,0:T(8,128)(2,1)}, bf16[3,4,1,32,1792]{4,3,2,1,0:T(8,128)(2,1)}, u32[]{:S(2)}, u32[]{:S(2)}) collective-permute-start(bf16[3,4,1,32,1792]{4,3,2,1,0:T(8,128)(2,1)} %pack.132.refs_2_), channel_id=1, source_target_pairs={{0,2},{2,0},{4,6},{6,4},{1,3},{3,1},{5,7},{7,5},{8,10},{10,8},{12,... | collective-permute-start | bytes 4128776 | tf_op jit(solution)/shard_map/cond/branch_1_fun/ppermute | solution.py:514
  175.5 60.6 %collective-permute-start.53 = (bf16[3,4,1,32,1792]{4,3,2,1,0:T(8,128)(2,1)}, bf16[3,4,1,32,1792]{4,3,2,1,0:T(8,128)(2,1)}, u32[]{:S(2)}, u32[]{:S(2)}) collective-permute-start(bf16[3,4,1,32,1792]{4,3,2,1,0:T(8,128)(2,1)} %pack.131.refs_3_), channel_id=1, source_target_pairs={{2,4},{4,2},{0,1},{6,7},{3,5},{5,3},{1,0},{7,6},{10,12},{12,10},{8... | collective-permute-start | bytes 4128776 | tf_op jit(solution)/shard_map/cond/branch_1_fun/ppermute | solution.py:488
  205.2 51.1 %collective-permute-start.50 = (bf16[3,4,1,32,1792]{4,3,2,1,0:T(8,128)(2,1)}, bf16[3,4,1,32,1792]{4,3,2,1,0:T(8,128)(2,1)S(1)}, u32[]{:S(2)}, u32[]{:S(2)}) collective-permute-start(bf16[3,4,1,32,1792]{4,3,2,1,0:T(8,128)(2,1)} %pack.135.refs_0_), channel_id=1, source_target_pairs={{0,2},{2,0},{4,6},{6,4},{1,3},{3,1},{5,7},{7,5},{8,10},{10,8},{12,... | collective-permute-start | bytes 4128776 | tf_op jit(solution)/shard_map/cond/branch_1_fun/ppermute | solution.py:514
  209.7 50.9 %collective-permute-start.56 = (bf16[3,4,1,32,1792]{4,3,2,1,0:T(8,128)(2,1)}, bf16[3,4,1,32,1792]{4,3,2,1,0:T(8,128)(2,1)}, u32[]{:S(2)}, u32[]{:S(2)}) collective-permute-start(bf16[3,4,1,32,1792]{4,3,2,1,0:T(8,128)(2,1)} %pack.134.refs_2_), channel_id=1, source_target_pairs={{2,4},{4,2},{0,1},{6,7},{3,5},{5,3},{1,0},{7,6},{10,12},{12,10},{8... | collective-permute-start | bytes 4128776 | tf_op jit(solution)/shard_map/cond/branch_1_fun/ppermute | solution.py:488
  241.4 44.4 %collective-permute-start.59 = (bf16[3,4,1,32,1792]{4,3,2,1,0:T(8,128)(2,1)S(1)}, bf16[3,4,1,32,1792]{4,3,2,1,0:T(8,128)(2,1)S(1)}, u32[]{:S(2)}, u32[]{:S(2)}) collective-permute-start(bf16[3,4,1,32,1792]{4,3,2,1,0:T(8,128)(2,1)S(1)} %pack.138.refs_2_), channel_id=1, source_target_pairs={{0,2},{2,0},{4,6},{6,4},{1,3},{3,1},{5,7},{7,5},{8,10},{10,8},{12,... | collective-permute-start | bytes 4128776 | tf_op jit(solution)/shard_map/cond/branch_1_fun/ppermute | solution.py:514
  242.8 49.8 %collective-permute-start.61 = (bf16[3,4,1,32,1792]{4,3,2,1,0:T(8,128)(2,1)}, bf16[3,4,1,32,1792]{4,3,2,1,0:T(8,128)(2,1)S(1)}, u32[]{:S(2)}, u32[]{:S(2)}) collective-permute-start(bf16[3,4,1,32,1792]{4,3,2,1,0:T(8,128)(2,1)} %pack.137.refs_2_), channel_id=1, source_target_pairs={{2,4},{4,2},{0,1},{6,7},{3,5},{5,3},{1,0},{7,6},{10,12},{12,10},{8... | collective-permute-start | bytes 4128776 | tf_op jit(solution)/shard_map/cond/branch_1_fun/ppermute | solution.py:488
  242.8 55.7 %collective-permute-start.60 = (bf16[3,4,1,32,1792]{4,3,2,1,0:T(8,128)(2,1)}, bf16[3,4,1,32,1792]{4,3,2,1,0:T(8,128)(2,1)}, u32[]{:S(2)}, u32[]{:S(2)}) collective-permute-start(bf16[3,4,1,32,1792]{4,3,2,1,0:T(8,128)(2,1)} %pack.136.refs_1_), channel_id=1, source_target_pairs={{0,1},{2,3},{4,5},{6,7},{1,0},{3,2},{5,4},{7,6},{8,9},{10,11},{12,... | collective-permute-start | bytes 4128776 | tf_op jit(solution)/shard_map/cond/branch_1_fun/ppermute | solution.py:404
  273.8 41.5 %collective-permute-start.58 = (bf16[3,4,1,32,1792]{4,3,2,1,0:T(8,128)(2,1)}, bf16[3,4,1,32,1792]{4,3,2,1,0:T(8,128)(2,1)S(1)}, u32[]{:S(2)}, u32[]{:S(2)}) collective-permute-start(bf16[3,4,1,32,1792]{4,3,2,1,0:T(8,128)(2,1)} %pack.141.refs_0_), channel_id=1, source_target_pairs={{0,2},{2,0},{4,6},{6,4},{1,3},{3,1},{5,7},{7,5},{8,10},{10,8},{12,... | collective-permute-start | bytes 4128776 | tf_op jit(solution)/shard_map/cond/branch_1_fun/ppermute | solution.py:514
  274.9 43.3 %collective-permute-start.57 = (bf16[3,4,1,32,1792]{4,3,2,1,0:T(8,128)(2,1)}, bf16[3,4,1,32,1792]{4,3,2,1,0:T(8,128)(2,1)}, u32[]{:S(2)}, u32[]{:S(2)}) collective-permute-start(bf16[3,4,1,32,1792]{4,3,2,1,0:T(8,128)(2,1)} %pack.140.refs_3_), channel_id=1, source_target_pairs={{2,4},{4,2},{0,1},{6,7},{3,5},{5,3},{1,0},{7,6},{10,12},{12,10},{8... | collective-permute-start | bytes 4128776 | tf_op jit(solution)/shard_map/cond/branch_1_fun/ppermute | solution.py:488
  285.7 42.4 %collective-permute-start.55 = (bf16[3,4,1,32,1792]{4,3,2,1,0:T(8,128)(2,1)}, bf16[3,4,1,32,1792]{4,3,2,1,0:T(8,128)(2,1)}, u32[]{:S(2)}, u32[]{:S(2)}) collective-permute-start(bf16[3,4,1,32,1792]{4,3,2,1,0:T(8,128)(2,1)} %pack.139.refs_1_), channel_id=1, source_target_pairs={{0,1},{2,3},{4,5},{6,7},{1,0},{3,2},{5,4},{7,6},{8,9},{10,11},{12,... | collective-permute-start | bytes 4128776 | tf_op jit(solution)/shard_map/cond/branch_1_fun/ppermute | solution.py:404
  298.4 46.4 %collective-permute-start.68 = (bf16[3,4,1,32,1792]{4,3,2,1,0:T(8,128)(2,1)}, bf16[3,4,1,32,1792]{4,3,2,1,0:T(8,128)(2,1)S(1)}, u32[]{:S(2)}, u32[]{:S(2)}) collective-permute-start(bf16[3,4,1,32,1792]{4,3,2,1,0:T(8,128)(2,1)} %pack.144.refs_4_), channel_id=1, source_target_pairs={{0,2},{2,0},{4,6},{6,4},{1,3},{3,1},{5,7},{7,5},{8,10},{10,8},{12,... | collective-permute-start | bytes 4128776 | tf_op jit(solution)/shard_map/cond/branch_1_fun/ppermute | solution.py:514
  298.5 49.9 %collective-permute-start.67 = (bf16[3,4,1,32,1792]{4,3,2,1,0:T(8,128)(2,1)}, bf16[3,4,1,32,1792]{4,3,2,1,0:T(8,128)(2,1)}, u32[]{:S(2)}, u32[]{:S(2)}) collective-permute-start(bf16[3,4,1,32,1792]{4,3,2,1,0:T(8,128)(2,1)} %pack.143.refs_4_), channel_id=1, source_target_pairs={{2,4},{4,2},{0,1},{6,7},{3,5},{5,3},{1,0},{7,6},{10,12},{12,10},{8... | collective-permute-start | bytes 4128776 | tf_op jit(solution)/shard_map/cond/branch_1_fun/ppermute | solution.py:488
  320.9 54.8 %collective-permute-start.64 = (bf16[3,4,1,32,1792]{4,3,2,1,0:T(8,128)(2,1)}, bf16[3,4,1,32,1792]{4,3,2,1,0:T(8,128)(2,1)}, u32[]{:S(2)}, u32[]{:S(2)}) collective-permute-start(bf16[3,4,1,32,1792]{4,3,2,1,0:T(8,128)(2,1)} %pack.146.refs_2_), channel_id=1, source_target_pairs={{2,4},{4,2},{0,1},{6,7},{3,5},{5,3},{1,0},{7,6},{10,12},{12,10},{8... | collective-permute-start | bytes 4128776 | tf_op jit(solution)/shard_map/cond/branch_1_fun/ppermute | solution.py:488
  351.3 59.9 %collective-permute-start.71 = (bf16[4,4,1,32,1792]{4,3,2,1,0:T(8,128)(2,1)}, bf16[4,4,1,32,1792]{4,3,2,1,0:T(8,128)(2,1)S(1)}, u32[]{:S(2)}, u32[]{:S(2)}) collective-permute-start(bf16[4,4,1,32,1792]{4,3,2,1,0:T(8,128)(2,1)} %pack.149.refs_2_), channel_id=1, source_target_pairs={{2,4},{4,2},{0,1},{6,7},{3,5},{5,3},{1,0},{7,6},{10,12},{12,10},{8... | collective-permute-start | bytes 5505032 | tf_op jit(solution)/shard_map/cond/branch_1_fun/ppermute | solution.py:488
  379.3 61.5 %collective-permute-start.78 = (bf16[3,4,1,32,1792]{4,3,2,1,0:T(8,128)(2,1)}, bf16[3,4,1,32,1792]{4,3,2,1,0:T(8,128)(2,1)}, u32[]{:S(2)}, u32[]{:S(2)}) collective-permute-start(bf16[3,4,1,32,1792]{4,3,2,1,0:T(8,128)(2,1)} %pack.152.refs_2_), channel_id=1, source_target_pairs={{2,4},{4,2},{0,1},{6,7},{3,5},{5,3},{1,0},{7,6},{10,12},{12,10},{8... | collective-permute-start | bytes 4128776 | tf_op jit(solution)/shard_map/cond/branch_1_fun/ppermute | solution.py:488
  (66 other events, 1005.4 us)
Sparse Core Ops, SparseCore 0:
  10.2 29.0 all-gather.1
  150.3 70.4 all-reduce.5

commit v2 on v1

--- a/solution.py
+++ b/solution.py
@@ -296,7 +296,7 @@
         if ride_due.get("out", n + 1) <= n and len(outs) < cap:
             outs.append(("ride", 0, 0))
             del ride_due["out"]
-        while fresh and opens[fresh[0][1]] <= n and len(outs) < cap:
+        while fresh and opens[fresh[0][1]] + (1 if opens[fresh[0][1]] == 5 else 0) <= n and len(outs) < cap:
             outs.append(fresh.pop(0))
         middle.append(across)
         inwards.append(ins)

time: 487 us -> 489 us (level)
  starting transfers between devices: 69.4 us -> 76.7 us
  waiting for transfers between devices: 172 us -> 167 us
    ppermute x12, waiting for transfers between devices: 59.3 us -> 53.1 us  [line_exchange(): got_middle[n] = lax.ppermute(packed(pieces, after), 'roll', middle_pairs)]
    ppermute x14, starting transfers between devices: 31.7 us -> 37 us  [swap(): lax.ppermute(packed([find(c, p, 'mate') for _, c, p in taken]), 'roll', s...]
    cond x83 -> x89, local copies, waits for them, and re-layouts: 9.79 us -> 8.74 us
where the time goes in v2:
time: 489 us; the launch traced here: 484 us
  Pallas kernels  205 us (42%)
  waiting for transfers between devices  167 us (34%)
  starting transfers between devices  76.7 us (16%)
  local copies, waits for them, and re-layouts  15.3 us (3%)
  between operations  14.7 us (3%)
    pallas_call x40, Pallas kernels, pack(): pl.pallas_call(functools.partial(pack_kernel, pieces, n_in), in_specs=[sm...  101 us
    ppermute x14, waiting for transfers between devices, line_exchange(): got_edge[n] = lax.ppermute(packed(pieces, after), 'roll', edge_pairs)  81.5 us
    pallas_call x22, Pallas kernels, place_pieces(): pl.pallas_call(functools.partial(place_kernel, pieces, sources, first, bl...  58.2 us
    ppermute x12, waiting for transfers between devices, line_exchange(): got_middle[n] = lax.ppermute(packed(pieces, after), 'roll', middle_pairs)  53.1 us
    ppermute x14, starting transfers between devices, swap(): lax.ppermute(packed([find(c, p, 'mate') for _, c, p in taken]), 'roll', s...  37 us
    pallas_call x3, Pallas kernels, quantize(): pl.pallas_call(functools.partial(quantize_kernel, trains), grid=(experts,...  26.3 us
    ppermute x14, starting transfers between devices, line_exchange(): got_edge[n] = lax.ppermute(packed(pieces, after), 'roll', edge_pairs)  18.1 us
    all_to_all x1, waiting for transfers between devices, per_device(): lax.all_to_all(quant, 'train', split_axis=0, concat_axis=0, tiled=True)  15.5 us
  transfers between devices with their start and end apart: 46, of which 18 were waited for; matrix products, arithmetic and copies ran while one was open for 1% of the time, Pallas kernels for 42%

profile of v2, /device:TPU:19, one launch (start us, length us, event | category | flops | bytes accessed | tf_op | source)
XLA Modules:
  0.0 484.4 jit_solution(16467890386610074912)
XLA Ops:
  9.6 8.3 %quantize.3 = (bf16[4,4,2,32,1792]{4,3,2,1,0:T(8,128)(2,1)S(1)}, bf16[4,2,128,1792]{3,2,1,0:T(8,128)(2,1)}) custom-call(f32[4,256,1792]{2,1,0:T(8,128)} %x_ref.3), custom_call_target="tpu_custom_call" | custom-call | flops 1 | bytes 1 | tf_op jit(solution)/shard_map/quantize/pallas_call | solution.py:42
  19.7 5.0 %all-to-all-start.4 = ((bf16[4,4,2,32,1792]{4,3,2,1,0:T(8,128)(2,1)}), bf16[4,4,2,32,1792]{4,3,2,1,0:T(8,128)(2,1)}, u32[]{:S(2)}, u32[]{:S(2)}) async-start(bf16[4,4,2,32,1792]{4,3,2,1,0:T(8,128)(2,1)} %copy-done.36), calls=%async_computation.4 | async-start | bytes 7340032 | tf_op jit(solution)/shard_map/all_to_all | solution.py:806
  26.0 8.3 %quantize.4 = (bf16[4,4,2,32,1792]{4,3,2,1,0:T(8,128)(2,1)S(1)}, bf16[4,2,128,1792]{3,2,1,0:T(8,128)(2,1)}) custom-call(f32[4,256,1792]{2,1,0:T(8,128)} %x_ref.4, s32[29]{0:T(128)S(1)} %plan.1.refs_0_), custom_call_target="tpu_custom_call" | custom-call | flops 1 | bytes 1 | tf_op jit(solution)/shard_map/quantize/pallas_call | solution.py:42
  34.3 9.7 %quantize.5 = (bf16[4,4,2,32,1792]{4,3,2,1,0:T(8,128)(2,1)}, bf16[4,2,128,1792]{3,2,1,0:T(8,128)(2,1)}) custom-call(f32[4,256,1792]{2,1,0:T(8,128)} %x_ref.5, bf16[4,4,2,32,1792]{4,3,2,1,0:T(8,128)(2,1)S(1)} %get-tuple-element.175.refs_0_), custom_call_target="tpu_custom_call" | custom-call | flops 1 | bytes 1 | tf_op jit(solution)/shard_map/quantize/pallas_call | solution.py:42
  50.0 15.5 %all-to-all-done.4 = bf16[4,4,2,32,1792]{4,3,2,1,0:T(8,128)(2,1)} async-done(((bf16[4,4,2,32,1792]{4,3,2,1,0:T(8,128)(2,1)}), bf16[4,4,2,32,1792]{4,3,2,1,0:T(8,128)(2,1)}, u32[]{:S(2)}, u32[]{:S(2)}) %all-to-all-start.4) | async-done | bytes 3670048 | tf_op jit(solution)/shard_map/all_to_all | solution.py:806
  65.6 410.8 %conditional.1 = (bf16[16,32,7168]{2,1,0:T(8,128)(2,1)}, bf16[16,32,7168]{2,1,0:T(8,128)(2,1)}, bf16[16,32,7168]{2,1,0:T(8,128)(2,1)}, bf16[64,1792]{1,0:T(8,128)(2,1)}) conditional(s32[]{:T(128)} %bitcast.17, (s32[29]{0:T(128)S(1)}, bf16[4,4,2,32,1792]{4,3,2,1,0:T(8,128)(2,1)}, bf16[512,1792]{1,0:T(8,128)(2,1)}, s32[512,2]{1,0:T(8,128)S(1)}, ...), branch_computations={%region_0.2_spmd, %region_2.4_spmd} | conditional | flops 524359 | bytes 473172832 | solution.py:819
  65.6 5.2 %all-to-all-start.2 = ((bf16[4,4,2,32,1792]{4,3,2,1,0:T(8,128)(2,1)}), bf16[4,4,2,32,1792]{4,3,2,1,0:T(8,128)(2,1)}, u32[]{:S(2)}, u32[]{:S(2)}) async-start(bf16[4,4,2,32,1792]{4,3,2,1,0:T(8,128)(2,1)} %get-tuple-element.103), calls=%async_computation.2 | async-start | bytes 7340032 | tf_op jit(solution)/shard_map/cond/branch_1_fun/all_to_all | solution.py:342
  91.8 12.0 %collective-permute-done.41.refs_0_.refs_2_ = bf16[3,4,1,32,1792]{4,3,2,1,0:T(8,128)(2,1)} collective-permute-done((bf16[3,4,1,32,1792]{4,3,2,1,0:T(8,128)(2,1)}, bf16[3,4,1,32,1792]{4,3,2,1,0:T(8,128)(2,1)}, u32[]{:S(2)}, u32[]{:S(2)}) %collective-permute-start.41) | collective-permute-done | bytes 1376288 | tf_op jit(solution)/shard_map/cond/branch_1_fun/ppermute | solution.py:488
  110.8 5.9 %all-to-all-start.3 = ((bf16[4,4,2,32,1792]{4,3,2,1,0:T(8,128)(2,1)}), bf16[4,4,2,32,1792]{4,3,2,1,0:T(8,128)(2,1)}, u32[]{:S(2)}, u32[]{:S(2)}) async-start(bf16[4,4,2,32,1792]{4,3,2,1,0:T(8,128)(2,1)} %get-tuple-element.104), calls=%async_computation.3 | async-start | bytes 7340032 | tf_op jit(solution)/shard_map/cond/branch_1_fun/all_to_all | solution.py:342
  127.8 10.6 %collective-permute-done.42.refs_1_.refs_0_.refs_3_ = bf16[3,4,1,32,1792]{4,3,2,1,0:T(8,128)(2,1)S(1)} collective-permute-done((bf16[3,4,1,32,1792]{4,3,2,1,0:T(8,128)(2,1)}, bf16[3,4,1,32,1792]{4,3,2,1,0:T(8,128)(2,1)S(1)}, u32[]{:S(2)}, u32[]{:S(2)}) %collective-permute-start.42) | collective-permute-done | bytes 1376288 | tf_op jit(solution)/shard_map/cond/branch_1_fun/ppermute | solution.py:514
  152.7 12.7 %collective-permute-done.48.refs_2_.refs_0_ = bf16[3,4,1,32,1792]{4,3,2,1,0:T(8,128)(2,1)} collective-permute-done((bf16[3,4,1,32,1792]{4,3,2,1,0:T(8,128)(2,1)}, bf16[3,4,1,32,1792]{4,3,2,1,0:T(8,128)(2,1)}, u32[]{:S(2)}, u32[]{:S(2)}) %collective-permute-start.48) | collective-permute-done | bytes 1376288 | tf_op jit(solution)/shard_map/cond/branch_1_fun/ppermute | solution.py:488
  183.4 14.0 %collective-permute-done.46.refs_1_.refs_0_.refs_4_ = bf16[3,4,1,32,1792]{4,3,2,1,0:T(8,128)(2,1)S(1)} collective-permute-done((bf16[3,4,1,32,1792]{4,3,2,1,0:T(8,128)(2,1)}, bf16[3,4,1,32,1792]{4,3,2,1,0:T(8,128)(2,1)S(1)}, u32[]{:S(2)}, u32[]{:S(2)}) %collective-permute-start.46) | collective-permute-done | bytes 1376288 | tf_op jit(solution)/shard_map/cond/branch_1_fun/ppermute | solution.py:514
  209.8 11.0 %all-reduce.6.cloned.1.call-done.pre_ref = f32[512,1024]{1,0:T(8,128)} async-done(((f32[512,1024]{1,0:T(8,128)}), f32[512,1024]{1,0:T(8,128)}) %all-reduce.6.cloned.1.call-update) | async-done | bytes 2097168 | tf_op jit(solution)/shard_map/cond/branch_1_fun/psum | solution.py:433
  222.4 7.1 %mix_experts.3 = (f32[4,64,1792]{2,1,0:T(8,128)S(1)}, bf16[256,1792]{1,0:T(8,128)(2,1)S(1)}) custom-call(f32[512,1024]{1,0:T(8,128)S(1)} %copy-done.53, s32[512,2]{1,0:T(8,128)S(1)} %copy-done.91, f32[512,2]{1,0:T(8,128)} %get-tuple-element.108.weights_ref, bf16[4,2,128,1792]{3,2,1,0:T(8,128)(2,1)} %get-tuple-element.109.down_ref, ...), custom_call_target="tpu_custom_call" | custom-call | flops 1 | bytes 1 | tf_op jit(solution)/shard_map/cond/branch_1_fun/mix_experts/pallas_call | solution.py:658
  243.4 12.9 %collective-permute-done.50.refs_3_.refs_0_.refs_4_.refs_1_ = bf16[3,4,1,32,1792]{4,3,2,1,0:T(8,128)(2,1)S(1)} collective-permute-done((bf16[3,4,1,32,1792]{4,3,2,1,0:T(8,128)(2,1)}, bf16[3,4,1,32,1792]{4,3,2,1,0:T(8,128)(2,1)S(1)}, u32[]{:S(2)}, u32[]{:S(2)}) %collective-permute-start.50) | collective-permute-done | bytes 1376288 | tf_op jit(solution)/shard_map/cond/branch_1_fun/ppermute | solution.py:514
  275.9 9.9 %collective-permute-done.59.refs_2_.refs_0_.refs_5_.refs_1_ = bf16[3,4,1,32,1792]{4,3,2,1,0:T(8,128)(2,1)S(1)} collective-permute-done((bf16[3,4,1,32,1792]{4,3,2,1,0:T(8,128)(2,1)}, bf16[3,4,1,32,1792]{4,3,2,1,0:T(8,128)(2,1)S(1)}, u32[]{:S(2)}, u32[]{:S(2)}) %collective-permute-start.59) | collective-permute-done | bytes 1376288 | tf_op jit(solution)/shard_map/cond/branch_1_fun/ppermute | solution.py:514
  285.8 4.2 collective-permute-start.55
  306.9 8.4 %collective-permute-done.58.refs_1_.refs_4_.refs_3_ = bf16[3,4,1,32,1792]{4,3,2,1,0:T(8,128)(2,1)S(1)} collective-permute-done((bf16[3,4,1,32,1792]{4,3,2,1,0:T(8,128)(2,1)}, bf16[3,4,1,32,1792]{4,3,2,1,0:T(8,128)(2,1)S(1)}, u32[]{:S(2)}, u32[]{:S(2)}) %collective-permute-start.58) | collective-permute-done | bytes 1376288 | tf_op jit(solution)/shard_map/cond/branch_1_fun/ppermute | solution.py:514
  336.9 7.9 %collective-permute-done.66.refs_1_.refs_3_.refs_4_.refs_2_ = bf16[3,4,1,32,1792]{4,3,2,1,0:T(8,128)(2,1)S(1)} collective-permute-done((bf16[3,4,1,32,1792]{4,3,2,1,0:T(8,128)(2,1)}, bf16[3,4,1,32,1792]{4,3,2,1,0:T(8,128)(2,1)S(1)}, u32[]{:S(2)}, u32[]{:S(2)}) %collective-permute-start.66) | collective-permute-done | bytes 1376288 | tf_op jit(solution)/shard_map/cond/branch_1_fun/ppermute | solution.py:514
  350.4 4.6 collective-permute-start.73
  362.8 11.5 %collective-permute-done.65.refs_1_.refs_3_ = bf16[3,4,1,32,1792]{4,3,2,1,0:T(8,128)(2,1)S(1)} collective-permute-done((bf16[3,4,1,32,1792]{4,3,2,1,0:T(8,128)(2,1)}, bf16[3,4,1,32,1792]{4,3,2,1,0:T(8,128)(2,1)S(1)}, u32[]{:S(2)}, u32[]{:S(2)}) %collective-permute-start.65) | collective-permute-done | bytes 1376288 | tf_op jit(solution)/shard_map/cond/branch_1_fun/ppermute | solution.py:514
  395.8 15.4 %collective-permute-done.71.refs_0_ = bf16[4,4,1,32,1792]{4,3,2,1,0:T(8,128)(2,1)S(1)} collective-permute-done((bf16[4,4,1,32,1792]{4,3,2,1,0:T(8,128)(2,1)}, bf16[4,4,1,32,1792]{4,3,2,1,0:T(8,128)(2,1)S(1)}, u32[]{:S(2)}, u32[]{:S(2)}) %collective-permute-start.71) | collective-permute-done | bytes 1835040 | tf_op jit(solution)/shard_map/cond/branch_1_fun/ppermute | solution.py:488
  414.6 6.7 %collective-permute-start.70 = (bf16[1,4,1,32,1792]{4,3,2,1,0:T(8,128)(2,1)S(1)}, bf16[1,4,1,32,1792]{4,3,2,1,0:T(8,128)(2,1)S(1)}, u32[]{:S(2)}, u32[]{:S(2)}) collective-permute-start(bf16[1,4,1,32,1792]{4,3,2,1,0:T(8,128)(2,1)S(1)} %copy-done.65), channel_id=1, source_target_pairs={{0,1},{2,3},{4,5},{6,7},{1,0},{3,2},{5,4},{7,6},{8,9},{10,11},{12,... | collective-permute-start | bytes 1376264 | tf_op jit(solution)/shard_map/cond/branch_1_fun/ppermute | solution.py:404
  427.7 13.0 %collective-permute-done.78.refs_0_ = bf16[3,4,1,32,1792]{4,3,2,1,0:T(8,128)(2,1)} collective-permute-done((bf16[3,4,1,32,1792]{4,3,2,1,0:T(8,128)(2,1)}, bf16[3,4,1,32,1792]{4,3,2,1,0:T(8,128)(2,1)}, u32[]{:S(2)}, u32[]{:S(2)}) %collective-permute-start.78) | collective-permute-done | bytes 1376288 | tf_op jit(solution)/shard_map/cond/branch_1_fun/ppermute | solution.py:488
  (253 shorter events, 248.4 us)
Async XLA Ops:
  19.7 45.9 %all-to-all-start.4 = ((bf16[4,4,2,32,1792]{4,3,2,1,0:T(8,128)(2,1)}), bf16[4,4,2,32,1792]{4,3,2,1,0:T(8,128)(2,1)}, u32[]{:S(2)}, u32[]{:S(2)}) async-start(bf16[4,4,2,32,1792]{4,3,2,1,0:T(8,128)(2,1)} %copy-done.36), calls=%async_computation.4 | async-start | bytes 7340032 | tf_op jit(solution)/shard_map/all_to_all | solution.py:806
  65.6 45.3 %all-to-all-start.2 = ((bf16[4,4,2,32,1792]{4,3,2,1,0:T(8,128)(2,1)}), bf16[4,4,2,32,1792]{4,3,2,1,0:T(8,128)(2,1)}, u32[]{:S(2)}, u32[]{:S(2)}) async-start(bf16[4,4,2,32,1792]{4,3,2,1,0:T(8,128)(2,1)} %get-tuple-element.103), calls=%async_computation.2 | async-start | bytes 7340032 | tf_op jit(solution)/shard_map/cond/branch_1_fun/all_to_all | solution.py:342
  76.7 42.6 %collective-permute-start.43 = (bf16[3,4,1,32,1792]{4,3,2,1,0:T(8,128)(2,1)}, bf16[3,4,1,32,1792]{4,3,2,1,0:T(8,128)(2,1)S(1)}, u32[]{:S(2)}, u32[]{:S(2)}) collective-permute-start(bf16[3,4,1,32,1792]{4,3,2,1,0:T(8,128)(2,1)} %pack.121.refs_0_), channel_id=1, source_target_pairs={{0,2},{2,0},{4,6},{6,4},{1,3},{3,1},{5,7},{7,5},{8,10},{10,8},{12,... | collective-permute-start | bytes 4128776 | tf_op jit(solution)/shard_map/cond/branch_1_fun/ppermute | solution.py:514
  110.8 91.6 %all-to-all-start.3 = ((bf16[4,4,2,32,1792]{4,3,2,1,0:T(8,128)(2,1)}), bf16[4,4,2,32,1792]{4,3,2,1,0:T(8,128)(2,1)}, u32[]{:S(2)}, u32[]{:S(2)}) async-start(bf16[4,4,2,32,1792]{4,3,2,1,0:T(8,128)(2,1)} %get-tuple-element.104), calls=%async_computation.3 | async-start | bytes 7340032 | tf_op jit(solution)/shard_map/cond/branch_1_fun/all_to_all | solution.py:342
  116.7 104.1 %all-reduce.6.cloned.1.call-start = ((), (), s32[]{:S(2)}) async-start(), calls=%async_computation.6 | async-start | bytes 4194304 | tf_op jit(solution)/shard_map/cond/branch_1_fun/psum | solution.py:433
  121.8 43.6 %collective-permute-start.48 = (bf16[3,4,1,32,1792]{4,3,2,1,0:T(8,128)(2,1)}, bf16[3,4,1,32,1792]{4,3,2,1,0:T(8,128)(2,1)}, u32[]{:S(2)}, u32[]{:S(2)}) collective-permute-start(bf16[3,4,1,32,1792]{4,3,2,1,0:T(8,128)(2,1)} %pack.125.refs_1_), channel_id=1, source_target_pairs={{2,4},{4,2},{0,1},{6,7},{3,5},{5,3},{1,0},{7,6},{10,12},{12,10},{8... | collective-permute-start | bytes 4128776 | tf_op jit(solution)/shard_map/cond/branch_1_fun/ppermute | solution.py:488
  124.8 43.1 %collective-permute-start.49 = (bf16[3,4,1,32,1792]{4,3,2,1,0:T(8,128)(2,1)}, bf16[3,4,1,32,1792]{4,3,2,1,0:T(8,128)(2,1)}, u32[]{:S(2)}, u32[]{:S(2)}) collective-permute-start(bf16[3,4,1,32,1792]{4,3,2,1,0:T(8,128)(2,1)} %pack.126.refs_2_), channel_id=1, source_target_pairs={{0,2},{2,0},{4,6},{6,4},{1,3},{3,1},{5,7},{7,5},{8,10},{10,8},{12,... | collective-permute-start | bytes 4128776 | tf_op jit(solution)/shard_map/cond/branch_1_fun/ppermute | solution.py:514
  145.4 52.0 %collective-permute-start.46 = (bf16[3,4,1,32,1792]{4,3,2,1,0:T(8,128)(2,1)}, bf16[3,4,1,32,1792]{4,3,2,1,0:T(8,128)(2,1)S(1)}, u32[]{:S(2)}, u32[]{:S(2)}) collective-permute-start(bf16[3,4,1,32,1792]{4,3,2,1,0:T(8,128)(2,1)} %pack.129.refs_1_), channel_id=1, source_target_pairs={{0,2},{2,0},{4,6},{6,4},{1,3},{3,1},{5,7},{7,5},{8,10},{10,8},{12,... | collective-permute-start | bytes 4128776 | tf_op jit(solution)/shard_map/cond/branch_1_fun/ppermute | solution.py:514
  146.9 52.3 %collective-permute-start.45 = (bf16[3,4,1,32,1792]{4,3,2,1,0:T(8,128)(2,1)}, bf16[3,4,1,32,1792]{4,3,2,1,0:T(8,128)(2,1)}, u32[]{:S(2)}, u32[]{:S(2)}) collective-permute-start(bf16[3,4,1,32,1792]{4,3,2,1,0:T(8,128)(2,1)} %pack.128.refs_2_), channel_id=1, source_target_pairs={{2,4},{4,2},{0,1},{6,7},{3,5},{5,3},{1,0},{7,6},{10,12},{12,10},{8... | collective-permute-start | bytes 4128776 | tf_op jit(solution)/shard_map/cond/branch_1_fun/ppermute | solution.py:488
  173.3 59.4 %collective-permute-start.51 = (bf16[3,4,1,32,1792]{4,3,2,1,0:T(8,128)(2,1)}, bf16[3,4,1,32,1792]{4,3,2,1,0:T(8,128)(2,1)}, u32[]{:S(2)}, u32[]{:S(2)}) collective-permute-start(bf16[3,4,1,32,1792]{4,3,2,1,0:T(8,128)(2,1)} %pack.132.refs_2_), channel_id=1, source_target_pairs={{0,2},{2,0},{4,6},{6,4},{1,3},{3,1},{5,7},{7,5},{8,10},{10,8},{12,... | collective-permute-start | bytes 4128776 | tf_op jit(solution)/shard_map/cond/branch_1_fun/ppermute | solution.py:514
  175.5 59.9 %collective-permute-start.53 = (bf16[3,4,1,32,1792]{4,3,2,1,0:T(8,128)(2,1)}, bf16[3,4,1,32,1792]{4,3,2,1,0:T(8,128)(2,1)}, u32[]{:S(2)}, u32[]{:S(2)}) collective-permute-start(bf16[3,4,1,32,1792]{4,3,2,1,0:T(8,128)(2,1)} %pack.131.refs_3_), channel_id=1, source_target_pairs={{2,4},{4,2},{0,1},{6,7},{3,5},{5,3},{1,0},{7,6},{10,12},{12,10},{8... | collective-permute-start | bytes 4128776 | tf_op jit(solution)/shard_map/cond/branch_1_fun/ppermute | solution.py:488
  205.2 51.1 %collective-permute-start.50 = (bf16[3,4,1,32,1792]{4,3,2,1,0:T(8,128)(2,1)}, bf16[3,4,1,32,1792]{4,3,2,1,0:T(8,128)(2,1)S(1)}, u32[]{:S(2)}, u32[]{:S(2)}) collective-permute-start(bf16[3,4,1,32,1792]{4,3,2,1,0:T(8,128)(2,1)} %pack.135.refs_0_), channel_id=1, source_target_pairs={{0,2},{2,0},{4,6},{6,4},{1,3},{3,1},{5,7},{7,5},{8,10},{10,8},{12,... | collective-permute-start | bytes 4128776 | tf_op jit(solution)/shard_map/cond/branch_1_fun/ppermute | solution.py:514
  209.6 50.9 %collective-permute-start.56 = (bf16[3,4,1,32,1792]{4,3,2,1,0:T(8,128)(2,1)}, bf16[3,4,1,32,1792]{4,3,2,1,0:T(8,128)(2,1)}, u32[]{:S(2)}, u32[]{:S(2)}) collective-permute-start(bf16[3,4,1,32,1792]{4,3,2,1,0:T(8,128)(2,1)} %pack.134.refs_3_), channel_id=1, source_target_pairs={{2,4},{4,2},{0,1},{6,7},{3,5},{5,3},{1,0},{7,6},{10,12},{12,10},{8... | collective-permute-start | bytes 4128776 | tf_op jit(solution)/shard_map/cond/branch_1_fun/ppermute | solution.py:488
  240.9 44.9 %collective-permute-start.59 = (bf16[3,4,1,32,1792]{4,3,2,1,0:T(8,128)(2,1)}, bf16[3,4,1,32,1792]{4,3,2,1,0:T(8,128)(2,1)S(1)}, u32[]{:S(2)}, u32[]{:S(2)}) collective-permute-start(bf16[3,4,1,32,1792]{4,3,2,1,0:T(8,128)(2,1)} %pack.138.refs_2_), channel_id=1, source_target_pairs={{0,2},{2,0},{4,6},{6,4},{1,3},{3,1},{5,7},{7,5},{8,10},{10,8},{12,... | collective-permute-start | bytes 4128776 | tf_op jit(solution)/shard_map/cond/branch_1_fun/ppermute | solution.py:514
  242.3 52.8 %collective-permute-start.61 = (bf16[3,4,1,32,1792]{4,3,2,1,0:T(8,128)(2,1)}, bf16[3,4,1,32,1792]{4,3,2,1,0:T(8,128)(2,1)}, u32[]{:S(2)}, u32[]{:S(2)}) collective-permute-start(bf16[3,4,1,32,1792]{4,3,2,1,0:T(8,128)(2,1)} %pack.137.refs_2_), channel_id=1, source_target_pairs={{2,4},{4,2},{0,1},{6,7},{3,5},{5,3},{1,0},{7,6},{10,12},{12,10},{8... | collective-permute-start | bytes 4128776 | tf_op jit(solution)/shard_map/cond/branch_1_fun/ppermute | solution.py:488
  242.3 58.1 %collective-permute-start.60 = (bf16[3,4,1,32,1792]{4,3,2,1,0:T(8,128)(2,1)}, bf16[3,4,1,32,1792]{4,3,2,1,0:T(8,128)(2,1)}, u32[]{:S(2)}, u32[]{:S(2)}) collective-permute-start(bf16[3,4,1,32,1792]{4,3,2,1,0:T(8,128)(2,1)} %pack.136.refs_1_), channel_id=1, source_target_pairs={{0,1},{2,3},{4,5},{6,7},{1,0},{3,2},{5,4},{7,6},{8,9},{10,11},{12,... | collective-permute-start | bytes 4128776 | tf_op jit(solution)/shard_map/cond/branch_1_fun/ppermute | solution.py:404
  273.8 44.3 %collective-permute-start.57 = (bf16[3,4,1,32,1792]{4,3,2,1,0:T(8,128)(2,1)}, bf16[3,4,1,32,1792]{4,3,2,1,0:T(8,128)(2,1)S(1)}, u32[]{:S(2)}, u32[]{:S(2)}) collective-permute-start(bf16[3,4,1,32,1792]{4,3,2,1,0:T(8,128)(2,1)} %pack.140.refs_3_), channel_id=1, source_target_pairs={{2,4},{4,2},{0,1},{6,7},{3,5},{5,3},{1,0},{7,6},{10,12},{12,10},{8... | collective-permute-start | bytes 4128776 | tf_op jit(solution)/shard_map/cond/branch_1_fun/ppermute | solution.py:488
  300.4 44.4 %collective-permute-start.66 = (bf16[3,4,1,32,1792]{4,3,2,1,0:T(8,128)(2,1)}, bf16[3,4,1,32,1792]{4,3,2,1,0:T(8,128)(2,1)S(1)}, u32[]{:S(2)}, u32[]{:S(2)}) collective-permute-start(bf16[3,4,1,32,1792]{4,3,2,1,0:T(8,128)(2,1)} %pack.144.refs_4_), channel_id=1, source_target_pairs={{0,2},{2,0},{4,6},{6,4},{1,3},{3,1},{5,7},{7,5},{8,10},{10,8},{12,... | collective-permute-start | bytes 4128776 | tf_op jit(solution)/shard_map/cond/branch_1_fun/ppermute | solution.py:514
  300.5 47.0 %collective-permute-start.68 = (bf16[3,4,1,32,1792]{4,3,2,1,0:T(8,128)(2,1)}, bf16[3,4,1,32,1792]{4,3,2,1,0:T(8,128)(2,1)}, u32[]{:S(2)}, u32[]{:S(2)}) collective-permute-start(bf16[3,4,1,32,1792]{4,3,2,1,0:T(8,128)(2,1)} %pack.143.refs_4_), channel_id=1, source_target_pairs={{2,4},{4,2},{0,1},{6,7},{3,5},{5,3},{1,0},{7,6},{10,12},{12,10},{8... | collective-permute-start | bytes 4128776 | tf_op jit(solution)/shard_map/cond/branch_1_fun/ppermute | solution.py:488
  324.2 50.1 %collective-permute-start.65 = (bf16[3,4,1,32,1792]{4,3,2,1,0:T(8,128)(2,1)}, bf16[3,4,1,32,1792]{4,3,2,1,0:T(8,128)(2,1)S(1)}, u32[]{:S(2)}, u32[]{:S(2)}) collective-permute-start(bf16[3,4,1,32,1792]{4,3,2,1,0:T(8,128)(2,1)} %pack.147.refs_3_), channel_id=1, source_target_pairs={{0,2},{2,0},{4,6},{6,4},{1,3},{3,1},{5,7},{7,5},{8,10},{10,8},{12,... | collective-permute-start | bytes 4128776 | tf_op jit(solution)/shard_map/cond/branch_1_fun/ppermute | solution.py:514
  325.9 51.2 %collective-permute-start.64 = (bf16[3,4,1,32,1792]{4,3,2,1,0:T(8,128)(2,1)}, bf16[3,4,1,32,1792]{4,3,2,1,0:T(8,128)(2,1)}, u32[]{:S(2)}, u32[]{:S(2)}) collective-permute-start(bf16[3,4,1,32,1792]{4,3,2,1,0:T(8,128)(2,1)} %pack.146.refs_3_), channel_id=1, source_target_pairs={{2,4},{4,2},{0,1},{6,7},{3,5},{5,3},{1,0},{7,6},{10,12},{12,10},{8... | collective-permute-start | bytes 4128776 | tf_op jit(solution)/shard_map/cond/branch_1_fun/ppermute | solution.py:488
  350.3 60.9 %collective-permute-start.71 = (bf16[4,4,1,32,1792]{4,3,2,1,0:T(8,128)(2,1)}, bf16[4,4,1,32,1792]{4,3,2,1,0:T(8,128)(2,1)S(1)}, u32[]{:S(2)}, u32[]{:S(2)}) collective-permute-start(bf16[4,4,1,32,1792]{4,3,2,1,0:T(8,128)(2,1)} %pack.149.refs_2_), channel_id=1, source_target_pairs={{2,4},{4,2},{0,1},{6,7},{3,5},{5,3},{1,0},{7,6},{10,12},{12,10},{8... | collective-permute-start | bytes 5505032 | tf_op jit(solution)/shard_map/cond/branch_1_fun/ppermute | solution.py:488
  379.8 60.9 %collective-permute-start.78 = (bf16[3,4,1,32,1792]{4,3,2,1,0:T(8,128)(2,1)}, bf16[3,4,1,32,1792]{4,3,2,1,0:T(8,128)(2,1)}, u32[]{:S(2)}, u32[]{:S(2)}) collective-permute-start(bf16[3,4,1,32,1792]{4,3,2,1,0:T(8,128)(2,1)} %pack.152.refs_2_), channel_id=1, source_target_pairs={{2,4},{4,2},{0,1},{6,7},{3,5},{5,3},{1,0},{7,6},{10,12},{12,10},{8... | collective-permute-start | bytes 4128776 | tf_op jit(solution)/shard_map/cond/branch_1_fun/ppermute | solution.py:488
  382.4 42.9 %collective-permute-start.69 = (bf16[2,4,1,32,1792]{4,3,2,1,0:T(8,128)(2,1)}, bf16[2,4,1,32,1792]{4,3,2,1,0:T(8,128)(2,1)}, u32[]{:S(2)}, u32[]{:S(2)}) collective-permute-start(bf16[2,4,1,32,1792]{4,3,2,1,0:T(8,128)(2,1)} %pack.153.refs_5_), channel_id=1, source_target_pairs={{0,2},{2,0},{4,6},{6,4},{1,3},{3,1},{5,7},{7,5},{8,10},{10,8},{12,... | collective-permute-start | bytes 2752520 | tf_op jit(solution)/shard_map/cond/branch_1_fun/ppermute | solution.py:514
  (69 other events, 1008.7 us)
Sparse Core Ops, SparseCore 0:
  10.2 28.9 all-gather.1
  150.3 70.4 all-reduce.5
